TPU v7x, 32 devices: a whole 2x2x4 slice. The times are simulated.
32 devices in a mesh: slab: 4 (over x, core), tile: 8 (over z, y).
Axes of the slice: x: 2, y: 2, z: 4, core: 2. Of those that a mesh axis runs over, the one named last changes fastest.
Arguments:
- right_side: float32 [32, 128, 128], P('slab', 'tile'), may hold values from -8 to 8
- diagonal: float32 [32, 128, 128], P('slab', 'tile'), may hold values from 0.25 to 2
- inlet_index: int32 [4, 8, 32, 16], P('slab', 'tile'), may hold values from 0 to 16383
- plate_order: int32 [32], replicated, may hold values from 0 to 31, each once
- conductance: float32 [32], P('tile'), may hold values from 0.5 to 2
- plate_level: float32 [32], P('tile'), may hold values from -3 to 3
Outputs:
- solution: float32 [32, 128, 128], P('slab', 'tile')
- residual: float32 [32, 128, 128], P('slab', 'tile')
- inlet_flow: float32 [32], P('tile')
Inputs may be any that keep to these rules, and one draw needn't show every extreme that they name: `inlet_index`: each entry is a cell of the block of the device given by the first two indices. `plate_order`: each plate appears once.
All inputs are finite; a program needn't handle non-finite values.
Results may differ from a plain program's by a relative error of at most 0.0003.
Values sent between devices are 32-bit elements; how exact they have to be, the bound alone decides.
A program may use at most 64 MiB of HBM per device.

v0:
```python
import jax
import jax.numpy as jnp
from jax import lax
from jax.sharding import PartitionSpec as P

STEPS = 4
BLOCKS = 2


GRAM_PAIRS = [(row_at, col_at) for row_at in range(5) for col_at in range(row_at, 5)]


def extended(block, sides, width):
    for axis, dim in sides:
        count = lax.axis_size(axis)
        forward = [(i, i + 1) for i in range(count - 1)]
        backward = [(target, source) for source, target in forward]
        low = lax.ppermute(
            lax.slice_in_dim(block, block.shape[dim] - width, None, axis=dim), axis, forward
        )
        high = lax.ppermute(lax.slice_in_dim(block, 0, width, axis=dim), axis, backward)
        block = jnp.concatenate([low, block, high], axis=dim)
    return block


def apply_shifted(padded, diagonal):
    center = padded[1:-1, 1:-1]
    zero_col = jnp.zeros_like(center[:, :, :1])
    beside = padded[2:, 1:-1] + padded[:-2, 1:-1]
    beside = beside + padded[1:-1, 2:] + padded[1:-1, :-2]
    beside = (
        beside
        + jnp.concatenate([center[:, :, 1:], zero_col], axis=2)
        + jnp.concatenate([zero_col, center[:, :, :-1]], axis=2)
    )
    return ((diagonal - 1.0) * center - beside) / 7.0


def cholesky_solve(matrix, rhs):
    factor = jnp.linalg.cholesky(matrix)
    forward = []
    for row_at in range(4):
        value = rhs[row_at]
        for col_at in range(row_at):
            value = value - factor[row_at, col_at] * forward[col_at]
        forward.append(value / factor[row_at, row_at])
    backward = [None] * 4
    for row_at in range(3, -1, -1):
        value = forward[row_at]
        for col_at in range(row_at + 1, 4):
            value = value - factor[col_at, row_at] * backward[col_at]
        backward[row_at] = value / factor[row_at, row_at]
    return jnp.stack(backward)


def solve_block(gram_vec):
    entries = {}
    for place, pair in enumerate(GRAM_PAIRS):
        entries[pair] = gram_vec[place]
        entries[pair[1], pair[0]] = gram_vec[place]
    gram = jnp.stack(
        [jnp.stack([entries[row_at, col_at] for col_at in range(5)]) for row_at in range(5)]
    )
    matrix = 7.0 * (gram[:4, 1:] + gram[:4, :4])
    matrix = 0.5 * (matrix + matrix.T)
    return cholesky_solve(matrix, gram[:4, 0])


def update(solution, residual, basis, coeffs):
    for degree in range(4):
        solution = solution + coeffs[degree] * basis[degree]
        residual = residual - 7.0 * coeffs[degree] * (basis[degree + 1] + basis[degree])
    return (solution, residual)


def local_products(basis):
    stacked = jnp.stack(basis).reshape(len(basis), -1)
    full = jnp.dot(
        stacked, stacked.T, precision=lax.Precision.HIGHEST, preferred_element_type=jnp.float32
    )
    return jnp.stack([full[pair[0], pair[1]] for pair in GRAM_PAIRS])


def on_device(right_side, diagonal, inlet_index, plate_order, conductance, plate_level):
    solution = jnp.zeros_like(right_side)
    residual = right_side
    for repeat in range(BLOCKS):
        basis = [residual]
        for degree in range(STEPS):
            padded = extended(basis[-1], (("slab", 0), ("tile", 1)), 1)
            basis.append(apply_shifted(padded, diagonal))
        local_gram = local_products(basis)
        gram_vec = lax.psum(local_gram, ("slab", "tile"))
        coeffs = solve_block(gram_vec)
        solution, residual = update(solution, residual, basis, coeffs)
    flat_field = solution.reshape(-1)
    inlets = inlet_index.shape[3]
    picked = jnp.take(flat_field, inlet_index[0, 0], axis=0)
    contrib = jnp.sum(picked, axis=1)
    ordered = jnp.take(contrib, plate_order, axis=0)
    per_tile = conductance.shape[0]
    summed = lax.psum(ordered, ("slab", "tile"))
    owned = lax.dynamic_slice_in_dim(summed, lax.axis_index("tile") * per_tile, per_tile)
    scale = 1.0 / jnp.sqrt(jnp.float32(lax.axis_size("slab") * lax.axis_size("tile") * inlets))
    header = owned * scale
    inlet_flow = conductance * (header - plate_level)
    return (solution, residual, inlet_flow)


def solution(mesh):
    in_specs = (
        P("slab", "tile", None),
        P("slab", "tile", None),
        P("slab", "tile", None, None),
        P(),
        P("tile"),
        P("tile"),
    )
    out_specs = (P("slab", "tile", None), P("slab", "tile", None), P("tile"))
    return jax.shard_map(
        on_device, mesh=mesh, in_specs=in_specs, out_specs=out_specs, check_vma=False
    )
```

profile of v0, /device:TPU:0, one launch (start us, length us, event | category | flops | bytes accessed | tf_op | source)
XLA Modules:
  0.0 322.7 jit_solution(13443738939693373755)
XLA Ops:
  1.3 2.3 collective-permute-start.1
  5.9 2.9 collective-permute-done
  10.2 4.7 %collective-permute-start.3 = (f32[10,1,128]{2,1,0:T(1,128)S(1)}, f32[10,1,128]{2,1,0:T(1,128)S(1)}, u32[]{:S(2)}, u32[]{:S(2)}) collective-permute-start(f32[10,1,128]{2,1,0:T(1,128)S(1)} %get-tuple-element.35), channel_id=1, source_target_pairs={{0,1},{1,2},{2,3},{3,4},{4,5},{5,6},{6,7},{8,9},{9,10},{10,11},{11... | collective-permute-start | bytes 15368 | tf_op jit(solution)/shard_map/ppermute | solution.py:18
  17.6 3.8 %collective-permute-start.5 = (f32[1,16,128]{2,1,0:T(8,128)S(1)}, f32[1,16,128]{2,1,0:T(8,128)S(1)}, u32[]{:S(2)}, u32[]{:S(2)}) collective-permute-start(f32[1,16,128]{2,1,0:T(8,128)S(1)} %get-tuple-element.60), channel_id=1, source_target_pairs={{0,8},{8,16},{16,24},{1,9},{9,17},{17,25},{2,10},{10,18},{18,26},{... | collective-permute-start | bytes 24584 | tf_op jit(solution)/shard_map/ppermute | solution.py:18
  23.5 5.0 %collective-permute-start.7 = (f32[10,1,128]{2,1,0:T(1,128)S(1)}, f32[10,1,128]{2,1,0:T(1,128)S(1)}, u32[]{:S(2)}, u32[]{:S(2)}) collective-permute-start(f32[10,1,128]{2,1,0:T(1,128)S(1)} %get-tuple-element.33), channel_id=1, source_target_pairs={{0,1},{1,2},{2,3},{3,4},{4,5},{5,6},{6,7},{8,9},{9,10},{10,11},{11... | collective-permute-start | bytes 15368 | tf_op jit(solution)/shard_map/ppermute | solution.py:18
  31.2 3.4 %collective-permute-start.9 = (f32[1,16,128]{2,1,0:T(8,128)S(1)}, f32[1,16,128]{2,1,0:T(8,128)S(1)}, u32[]{:S(2)}, u32[]{:S(2)}) collective-permute-start(f32[1,16,128]{2,1,0:T(8,128)S(1)} %get-tuple-element.56), channel_id=1, source_target_pairs={{0,8},{8,16},{16,24},{1,9},{9,17},{17,25},{2,10},{10,18},{18,26},{... | collective-permute-start | bytes 24584 | tf_op jit(solution)/shard_map/ppermute | solution.py:18
  36.7 5.4 %collective-permute-start.11 = (f32[10,1,128]{2,1,0:T(1,128)S(1)}, f32[10,1,128]{2,1,0:T(1,128)S(1)}, u32[]{:S(2)}, u32[]{:S(2)}) collective-permute-start(f32[10,1,128]{2,1,0:T(1,128)S(1)} %get-tuple-element.31), channel_id=1, source_target_pairs={{0,1},{1,2},{2,3},{3,4},{4,5},{5,6},{6,7},{8,9},{9,10},{10,11},{11... | collective-permute-start | bytes 15368 | tf_op jit(solution)/shard_map/ppermute | solution.py:18
  44.9 4.8 %collective-permute-start.13 = (f32[1,16,128]{2,1,0:T(8,128)S(1)}, f32[1,16,128]{2,1,0:T(8,128)S(1)}, u32[]{:S(2)}, u32[]{:S(2)}) collective-permute-start(f32[1,16,128]{2,1,0:T(8,128)S(1)} %get-tuple-element.54), channel_id=1, source_target_pairs={{0,8},{8,16},{16,24},{1,9},{9,17},{17,25},{2,10},{10,18},{18,26},{... | collective-permute-start | bytes 24584 | tf_op jit(solution)/shard_map/ppermute | solution.py:18
  51.8 5.7 %collective-permute-start.15 = (f32[10,1,128]{2,1,0:T(1,128)S(1)}, f32[10,1,128]{2,1,0:T(1,128)S(1)}, u32[]{:S(2)}, u32[]{:S(2)}) collective-permute-start(f32[10,1,128]{2,1,0:T(1,128)S(1)} %get-tuple-element.29), channel_id=1, source_target_pairs={{0,1},{1,2},{2,3},{3,4},{4,5},{5,6},{6,7},{8,9},{9,10},{10,11},{11... | collective-permute-start | bytes 15368 | tf_op jit(solution)/shard_map/ppermute | solution.py:18
  61.5 9.5 %stack.112 = f32[15]{0:T(128)S(1)} concatenate(f32[1]{0:T(128)} %bitcast.10, f32[1]{0:T(128)} %bitcast.12, f32[1]{0:T(128)} %bitcast.13, f32[1]{0:T(128)} %bitcast.14, f32[1]{0:T(128)} %bitcast.15, f32[1]{0:T(128)} %bitcast.16, f32[1]{0:T(128)} %bitcast.17, f32[1]{0:T(128)} %bitcast.18, f32[1]{0:T(128)} %bitcast.19, f32[1]{0:T(128)} %bitcast.20, f32[1]{0:T(128)} %bitcast.21, ...), dimensions={0} | concatenate | bytes 120 | tf_op jit(solution)/shard_map/stack | solution.py:81
  71.0 48.2 %psum.21 = f32[15]{0:T(128)S(1)} all-reduce(f32[15]{0:T(128)S(1)} %stack.112), channel_id=1, replica_groups=mesh['slab'=4,'tile'=8] {'slab','tile'}, use_global_device_ids=true, to_apply=%region_0.0 | all-reduce | flops 15 | bytes 120 | tf_op jit(solution)/shard_map/psum | solution.py:93
  141.4 3.0 collective-permute-start.17
  146.5 4.8 %collective-permute-start.19 = (f32[10,1,128]{2,1,0:T(1,128)S(1)}, f32[10,1,128]{2,1,0:T(1,128)S(1)}, u32[]{:S(2)}, u32[]{:S(2)}) collective-permute-start(f32[10,1,128]{2,1,0:T(1,128)S(1)} %get-tuple-element.27), channel_id=1, source_target_pairs={{0,1},{1,2},{2,3},{3,4},{4,5},{5,6},{6,7},{8,9},{9,10},{10,11},{11... | collective-permute-start | bytes 15368 | tf_op jit(solution)/shard_map/ppermute | solution.py:18
  154.1 3.0 collective-permute-start.21
  159.3 5.4 %collective-permute-start.23 = (f32[10,1,128]{2,1,0:T(1,128)S(1)}, f32[10,1,128]{2,1,0:T(1,128)S(1)}, u32[]{:S(2)}, u32[]{:S(2)}) collective-permute-start(f32[10,1,128]{2,1,0:T(1,128)S(1)} %get-tuple-element.25), channel_id=1, source_target_pairs={{0,1},{1,2},{2,3},{3,4},{4,5},{5,6},{6,7},{8,9},{9,10},{10,11},{11... | collective-permute-start | bytes 15368 | tf_op jit(solution)/shard_map/ppermute | solution.py:18
  167.4 4.4 %collective-permute-start.25 = (f32[1,16,128]{2,1,0:T(8,128)S(1)}, f32[1,16,128]{2,1,0:T(8,128)S(1)}, u32[]{:S(2)}, u32[]{:S(2)}) collective-permute-start(f32[1,16,128]{2,1,0:T(8,128)S(1)} %get-tuple-element.40), channel_id=1, source_target_pairs={{0,8},{8,16},{16,24},{1,9},{9,17},{17,25},{2,10},{10,18},{18,26},{... | collective-permute-start | bytes 24584 | tf_op jit(solution)/shard_map/ppermute | solution.py:18
  174.0 5.3 %collective-permute-start.27 = (f32[10,1,128]{2,1,0:T(1,128)S(1)}, f32[10,1,128]{2,1,0:T(1,128)S(1)}, u32[]{:S(2)}, u32[]{:S(2)}) collective-permute-start(f32[10,1,128]{2,1,0:T(1,128)S(1)} %get-tuple-element.23), channel_id=1, source_target_pairs={{0,1},{1,2},{2,3},{3,4},{4,5},{5,6},{6,7},{8,9},{9,10},{10,11},{11... | collective-permute-start | bytes 15368 | tf_op jit(solution)/shard_map/ppermute | solution.py:18
  182.0 4.9 %collective-permute-start.29 = (f32[1,16,128]{2,1,0:T(8,128)S(1)}, f32[1,16,128]{2,1,0:T(8,128)S(1)}, u32[]{:S(2)}, u32[]{:S(2)}) collective-permute-start(f32[1,16,128]{2,1,0:T(8,128)S(1)} %get-tuple-element.36), channel_id=1, source_target_pairs={{0,8},{8,16},{16,24},{1,9},{9,17},{17,25},{2,10},{10,18},{18,26},{... | collective-permute-start | bytes 24584 | tf_op jit(solution)/shard_map/ppermute | solution.py:18
  189.1 5.7 %collective-permute-start.31 = (f32[10,1,128]{2,1,0:T(1,128)S(1)}, f32[10,1,128]{2,1,0:T(1,128)S(1)}, u32[]{:S(2)}, u32[]{:S(2)}) collective-permute-start(f32[10,1,128]{2,1,0:T(1,128)S(1)} %get-tuple-element.21), channel_id=1, source_target_pairs={{0,1},{1,2},{2,3},{3,4},{4,5},{5,6},{6,7},{8,9},{9,10},{10,11},{11... | collective-permute-start | bytes 15368 | tf_op jit(solution)/shard_map/ppermute | solution.py:18
  198.2 9.5 %stack.127 = f32[15]{0:T(128)S(1)} concatenate(f32[1]{0:T(128)} %bitcast.53, f32[1]{0:T(128)} %bitcast.55, f32[1]{0:T(128)} %bitcast.56, f32[1]{0:T(128)} %bitcast.57, f32[1]{0:T(128)} %bitcast.58, f32[1]{0:T(128)} %bitcast.59, f32[1]{0:T(128)} %bitcast.60, f32[1]{0:T(128)} %bitcast.61, f32[1]{0:T(128)} %bitcast.62, f32[1]{0:T(128)} %bitcast.63, f32[1]{0:T(128)} %bitcast.64, ...), dimensions={0} | concatenate | bytes 120 | tf_op jit(solution)/shard_map/stack | solution.py:81
  207.7 48.1 %psum.22 = f32[15]{0:T(128)S(1)} all-reduce(f32[15]{0:T(128)S(1)} %stack.127), channel_id=1, replica_groups=mesh['slab'=4,'tile'=8] {'slab','tile'}, use_global_device_ids=true, to_apply=%region_3.5 | all-reduce | flops 15 | bytes 120 | tf_op jit(solution)/shard_map/psum | solution.py:93
  258.7 2.0 maximum_bitcast_fusion.5
  276.8 3.1 gather_fusion
  280.9 40.6 %psum.23 = f32[32]{0:T(128)S(1)} all-reduce(f32[32]{0:T(128)S(1)} %and_select_fusion), channel_id=1, replica_groups=mesh['slab'=4,'tile'=8] {'slab','tile'}, use_global_device_ids=true, to_apply=%region_5.7 | all-reduce | flops 32 | bytes 256 | tf_op jit(solution)/shard_map/psum | solution.py:102
  (155 shorter events, 59.5 us)
Async XLA Ops:
  3.7 5.2 %collective-permute-start = (f32[1,16,128]{2,1,0:T(8,128)S(1)}, f32[1,16,128]{2,1,0:T(8,128)S(1)}, u32[]{:S(2)}, u32[]{:S(2)}) collective-permute-start(f32[1,16,128]{2,1,0:T(8,128)S(1)} %get-tuple-element.64), channel_id=1, source_target_pairs={{8,0},{16,8},{24,16},{9,1},{17,9},{25,17},{10,2},{18,10},{26,18},{... | collective-permute-start | bytes 24584 | tf_op jit(solution)/shard_map/ppermute | solution.py:21
  8.9 6.1 %collective-permute-start.2 = (f32[10,1,128]{2,1,0:T(1,128)S(1)}, f32[10,1,128]{2,1,0:T(1,128)S(1)}, u32[]{:S(2)}, u32[]{:S(2)}) collective-permute-start(f32[10,1,128]{2,1,0:T(1,128)S(1)} %get-tuple-element.34), channel_id=1, source_target_pairs={{1,0},{2,1},{3,2},{4,3},{5,4},{6,5},{7,6},{9,8},{10,9},{11,10},{12... | collective-permute-start | bytes 15368 | tf_op jit(solution)/shard_map/ppermute | solution.py:21
  10.2 6.0 %collective-permute-start.3 = (f32[10,1,128]{2,1,0:T(1,128)S(1)}, f32[10,1,128]{2,1,0:T(1,128)S(1)}, u32[]{:S(2)}, u32[]{:S(2)}) collective-permute-start(f32[10,1,128]{2,1,0:T(1,128)S(1)} %get-tuple-element.35), channel_id=1, source_target_pairs={{0,1},{1,2},{2,3},{3,4},{4,5},{5,6},{6,7},{8,9},{9,10},{10,11},{11... | collective-permute-start | bytes 15368 | tf_op jit(solution)/shard_map/ppermute | solution.py:18
  16.3 5.1 %collective-permute-start.4 = (f32[1,16,128]{2,1,0:T(8,128)S(1)}, f32[1,16,128]{2,1,0:T(8,128)S(1)}, u32[]{:S(2)}, u32[]{:S(2)}) collective-permute-start(f32[1,16,128]{2,1,0:T(8,128)S(1)} %get-tuple-element.61), channel_id=1, source_target_pairs={{8,0},{16,8},{24,16},{9,1},{17,9},{25,17},{10,2},{18,10},{26,18},{... | collective-permute-start | bytes 24584 | tf_op jit(solution)/shard_map/ppermute | solution.py:21
  22.2 6.3 %collective-permute-start.6 = (f32[10,1,128]{2,1,0:T(1,128)S(1)}, f32[10,1,128]{2,1,0:T(1,128)S(1)}, u32[]{:S(2)}, u32[]{:S(2)}) collective-permute-start(f32[10,1,128]{2,1,0:T(1,128)S(1)} %get-tuple-element.32), channel_id=1, source_target_pairs={{1,0},{2,1},{3,2},{4,3},{5,4},{6,5},{7,6},{9,8},{10,9},{11,10},{12... | collective-permute-start | bytes 15368 | tf_op jit(solution)/shard_map/ppermute | solution.py:21
  23.5 6.3 %collective-permute-start.7 = (f32[10,1,128]{2,1,0:T(1,128)S(1)}, f32[10,1,128]{2,1,0:T(1,128)S(1)}, u32[]{:S(2)}, u32[]{:S(2)}) collective-permute-start(f32[10,1,128]{2,1,0:T(1,128)S(1)} %get-tuple-element.33), channel_id=1, source_target_pairs={{0,1},{1,2},{2,3},{3,4},{4,5},{5,6},{6,7},{8,9},{9,10},{10,11},{11... | collective-permute-start | bytes 15368 | tf_op jit(solution)/shard_map/ppermute | solution.py:18
  35.4 6.8 %collective-permute-start.10 = (f32[10,1,128]{2,1,0:T(1,128)S(1)}, f32[10,1,128]{2,1,0:T(1,128)S(1)}, u32[]{:S(2)}, u32[]{:S(2)}) collective-permute-start(f32[10,1,128]{2,1,0:T(1,128)S(1)} %get-tuple-element.30), channel_id=1, source_target_pairs={{1,0},{2,1},{3,2},{4,3},{5,4},{6,5},{7,6},{9,8},{10,9},{11,10},{12... | collective-permute-start | bytes 15368 | tf_op jit(solution)/shard_map/ppermute | solution.py:21
  36.7 6.7 %collective-permute-start.11 = (f32[10,1,128]{2,1,0:T(1,128)S(1)}, f32[10,1,128]{2,1,0:T(1,128)S(1)}, u32[]{:S(2)}, u32[]{:S(2)}) collective-permute-start(f32[10,1,128]{2,1,0:T(1,128)S(1)} %get-tuple-element.31), channel_id=1, source_target_pairs={{0,1},{1,2},{2,3},{3,4},{4,5},{5,6},{6,7},{8,9},{9,10},{10,11},{11... | collective-permute-start | bytes 15368 | tf_op jit(solution)/shard_map/ppermute | solution.py:18
  43.6 6.1 %collective-permute-start.12 = (f32[1,16,128]{2,1,0:T(8,128)S(1)}, f32[1,16,128]{2,1,0:T(8,128)S(1)}, u32[]{:S(2)}, u32[]{:S(2)}) collective-permute-start(f32[1,16,128]{2,1,0:T(8,128)S(1)} %get-tuple-element.55), channel_id=1, source_target_pairs={{8,0},{16,8},{24,16},{9,1},{17,9},{25,17},{10,2},{18,10},{26,18},{... | collective-permute-start | bytes 24584 | tf_op jit(solution)/shard_map/ppermute | solution.py:21
  44.9 5.6 %collective-permute-start.13 = (f32[1,16,128]{2,1,0:T(8,128)S(1)}, f32[1,16,128]{2,1,0:T(8,128)S(1)}, u32[]{:S(2)}, u32[]{:S(2)}) collective-permute-start(f32[1,16,128]{2,1,0:T(8,128)S(1)} %get-tuple-element.54), channel_id=1, source_target_pairs={{0,8},{8,16},{16,24},{1,9},{9,17},{17,25},{2,10},{10,18},{18,26},{... | collective-permute-start | bytes 24584 | tf_op jit(solution)/shard_map/ppermute | solution.py:18
  50.5 7.1 %collective-permute-start.14 = (f32[10,1,128]{2,1,0:T(1,128)S(1)}, f32[10,1,128]{2,1,0:T(1,128)S(1)}, u32[]{:S(2)}, u32[]{:S(2)}) collective-permute-start(f32[10,1,128]{2,1,0:T(1,128)S(1)} %get-tuple-element.28), channel_id=1, source_target_pairs={{1,0},{2,1},{3,2},{4,3},{5,4},{6,5},{7,6},{9,8},{10,9},{11,10},{12... | collective-permute-start | bytes 15368 | tf_op jit(solution)/shard_map/ppermute | solution.py:21
  51.8 7.0 %collective-permute-start.15 = (f32[10,1,128]{2,1,0:T(1,128)S(1)}, f32[10,1,128]{2,1,0:T(1,128)S(1)}, u32[]{:S(2)}, u32[]{:S(2)}) collective-permute-start(f32[10,1,128]{2,1,0:T(1,128)S(1)} %get-tuple-element.29), channel_id=1, source_target_pairs={{0,1},{1,2},{2,3},{3,4},{4,5},{5,6},{6,7},{8,9},{9,10},{10,11},{11... | collective-permute-start | bytes 15368 | tf_op jit(solution)/shard_map/ppermute | solution.py:18
  145.2 6.2 %collective-permute-start.18 = (f32[10,1,128]{2,1,0:T(1,128)S(1)}, f32[10,1,128]{2,1,0:T(1,128)S(1)}, u32[]{:S(2)}, u32[]{:S(2)}) collective-permute-start(f32[10,1,128]{2,1,0:T(1,128)S(1)} %get-tuple-element.26), channel_id=1, source_target_pairs={{1,0},{2,1},{3,2},{4,3},{5,4},{6,5},{7,6},{9,8},{10,9},{11,10},{12... | collective-permute-start | bytes 15368 | tf_op jit(solution)/shard_map/ppermute | solution.py:21
  146.5 6.1 %collective-permute-start.19 = (f32[10,1,128]{2,1,0:T(1,128)S(1)}, f32[10,1,128]{2,1,0:T(1,128)S(1)}, u32[]{:S(2)}, u32[]{:S(2)}) collective-permute-start(f32[10,1,128]{2,1,0:T(1,128)S(1)} %get-tuple-element.27), channel_id=1, source_target_pairs={{0,1},{1,2},{2,3},{3,4},{4,5},{5,6},{6,7},{8,9},{9,10},{10,11},{11... | collective-permute-start | bytes 15368 | tf_op jit(solution)/shard_map/ppermute | solution.py:18
  158.0 6.8 %collective-permute-start.22 = (f32[10,1,128]{2,1,0:T(1,128)S(1)}, f32[10,1,128]{2,1,0:T(1,128)S(1)}, u32[]{:S(2)}, u32[]{:S(2)}) collective-permute-start(f32[10,1,128]{2,1,0:T(1,128)S(1)} %get-tuple-element.24), channel_id=1, source_target_pairs={{1,0},{2,1},{3,2},{4,3},{5,4},{6,5},{7,6},{9,8},{10,9},{11,10},{12... | collective-permute-start | bytes 15368 | tf_op jit(solution)/shard_map/ppermute | solution.py:21
  159.3 6.8 %collective-permute-start.23 = (f32[10,1,128]{2,1,0:T(1,128)S(1)}, f32[10,1,128]{2,1,0:T(1,128)S(1)}, u32[]{:S(2)}, u32[]{:S(2)}) collective-permute-start(f32[10,1,128]{2,1,0:T(1,128)S(1)} %get-tuple-element.25), channel_id=1, source_target_pairs={{0,1},{1,2},{2,3},{3,4},{4,5},{5,6},{6,7},{8,9},{9,10},{10,11},{11... | collective-permute-start | bytes 15368 | tf_op jit(solution)/shard_map/ppermute | solution.py:18
  166.1 5.8 %collective-permute-start.24 = (f32[1,16,128]{2,1,0:T(8,128)S(1)}, f32[1,16,128]{2,1,0:T(8,128)S(1)}, u32[]{:S(2)}, u32[]{:S(2)}) collective-permute-start(f32[1,16,128]{2,1,0:T(8,128)S(1)} %get-tuple-element.41), channel_id=1, source_target_pairs={{8,0},{16,8},{24,16},{9,1},{17,9},{25,17},{10,2},{18,10},{26,18},{... | collective-permute-start | bytes 24584 | tf_op jit(solution)/shard_map/ppermute | solution.py:21
  167.4 5.2 %collective-permute-start.25 = (f32[1,16,128]{2,1,0:T(8,128)S(1)}, f32[1,16,128]{2,1,0:T(8,128)S(1)}, u32[]{:S(2)}, u32[]{:S(2)}) collective-permute-start(f32[1,16,128]{2,1,0:T(8,128)S(1)} %get-tuple-element.40), channel_id=1, source_target_pairs={{0,8},{8,16},{16,24},{1,9},{9,17},{17,25},{2,10},{10,18},{18,26},{... | collective-permute-start | bytes 24584 | tf_op jit(solution)/shard_map/ppermute | solution.py:18
  172.7 6.7 %collective-permute-start.26 = (f32[10,1,128]{2,1,0:T(1,128)S(1)}, f32[10,1,128]{2,1,0:T(1,128)S(1)}, u32[]{:S(2)}, u32[]{:S(2)}) collective-permute-start(f32[10,1,128]{2,1,0:T(1,128)S(1)} %get-tuple-element.22), channel_id=1, source_target_pairs={{1,0},{2,1},{3,2},{4,3},{5,4},{6,5},{7,6},{9,8},{10,9},{11,10},{12... | collective-permute-start | bytes 15368 | tf_op jit(solution)/shard_map/ppermute | solution.py:21
  174.0 6.6 %collective-permute-start.27 = (f32[10,1,128]{2,1,0:T(1,128)S(1)}, f32[10,1,128]{2,1,0:T(1,128)S(1)}, u32[]{:S(2)}, u32[]{:S(2)}) collective-permute-start(f32[10,1,128]{2,1,0:T(1,128)S(1)} %get-tuple-element.23), channel_id=1, source_target_pairs={{0,1},{1,2},{2,3},{3,4},{4,5},{5,6},{6,7},{8,9},{9,10},{10,11},{11... | collective-permute-start | bytes 15368 | tf_op jit(solution)/shard_map/ppermute | solution.py:18
  180.7 6.3 %collective-permute-start.28 = (f32[1,16,128]{2,1,0:T(8,128)S(1)}, f32[1,16,128]{2,1,0:T(8,128)S(1)}, u32[]{:S(2)}, u32[]{:S(2)}) collective-permute-start(f32[1,16,128]{2,1,0:T(8,128)S(1)} %get-tuple-element.37), channel_id=1, source_target_pairs={{8,0},{16,8},{24,16},{9,1},{17,9},{25,17},{10,2},{18,10},{26,18},{... | collective-permute-start | bytes 24584 | tf_op jit(solution)/shard_map/ppermute | solution.py:21
  182.0 5.8 %collective-permute-start.29 = (f32[1,16,128]{2,1,0:T(8,128)S(1)}, f32[1,16,128]{2,1,0:T(8,128)S(1)}, u32[]{:S(2)}, u32[]{:S(2)}) collective-permute-start(f32[1,16,128]{2,1,0:T(8,128)S(1)} %get-tuple-element.36), channel_id=1, source_target_pairs={{0,8},{8,16},{16,24},{1,9},{9,17},{17,25},{2,10},{10,18},{18,26},{... | collective-permute-start | bytes 24584 | tf_op jit(solution)/shard_map/ppermute | solution.py:18
  187.8 7.0 %collective-permute-start.30 = (f32[10,1,128]{2,1,0:T(1,128)S(1)}, f32[10,1,128]{2,1,0:T(1,128)S(1)}, u32[]{:S(2)}, u32[]{:S(2)}) collective-permute-start(f32[10,1,128]{2,1,0:T(1,128)S(1)} %get-tuple-element.20), channel_id=1, source_target_pairs={{1,0},{2,1},{3,2},{4,3},{5,4},{6,5},{7,6},{9,8},{10,9},{11,10},{12... | collective-permute-start | bytes 15368 | tf_op jit(solution)/shard_map/ppermute | solution.py:21
  189.1 7.0 %collective-permute-start.31 = (f32[10,1,128]{2,1,0:T(1,128)S(1)}, f32[10,1,128]{2,1,0:T(1,128)S(1)}, u32[]{:S(2)}, u32[]{:S(2)}) collective-permute-start(f32[10,1,128]{2,1,0:T(1,128)S(1)} %get-tuple-element.21), channel_id=1, source_target_pairs={{0,1},{1,2},{2,3},{3,4},{4,5},{5,6},{6,7},{8,9},{9,10},{10,11},{11... | collective-permute-start | bytes 15368 | tf_op jit(solution)/shard_map/ppermute | solution.py:18
  (15 other events, 142.8 us)
where the time goes:
time: 325 us; the launch traced here: 323 us
  blocking collectives  137 us (42%)
  starting transfers between devices  92.4 us (28%)
  local copies, waits for them, and re-layouts  31.1 us (10%)
  between operations  27.5 us (8%)
  waiting for transfers between devices  18.1 us (6%)
  other arithmetic  14.1 us (4%)
    psum x2, blocking collectives, on_device(): gram_vec = lax.psum(local_gram, ('slab', 'tile'))  96.3 us
    ppermute x16, starting transfers between devices, extended(): lax.ppermute(lax.slice_in_dim(block, block.shape[dim] - width, None, axis...  71.7 us
    psum x1, blocking collectives, on_device(): summed = lax.psum(ordered, ('slab', 'tile'))  40.6 us
    ppermute x16, starting transfers between devices, extended(): lax.ppermute(lax.slice_in_dim(block, 0, width, axis=dim), axis, backward)  20.7 us
    another operation x2, local copies, waits for them, and re-layouts, local_products(): return jnp.stack([full[pair[0], pair[1]] for pair in GRAM_PAIRS])  19 us
    ppermute x16, waiting for transfers between devices, extended(): lax.ppermute(lax.slice_in_dim(block, block.shape[dim] - width, None, axis...  15.2 us
    another operation x7, other arithmetic, solve_block(): jnp.stack([jnp.stack([entries[row_at, col_at] for col_at in range(5)]) fo...  8.13 us
  transfers between devices with their start and end apart: 32, of which 16 were waited for; matrix products, arithmetic and copies ran while one was open for 1% of the time, Pallas kernels for 0%

commit v1 on v0

v1 whole, which is shorter than its diff:
```python
import functools

import jax
import jax.numpy as jnp
from jax import lax
from jax.experimental import pallas as pl
from jax.experimental.pallas import tpu as pltpu
from jax.sharding import PartitionSpec as P

STEPS = 4
HALO = 4
PAD = 8
MESH = pl.DeviceIdType.MESH
PAIRS = [(i, j) for i in range(5) for j in range(i, 5)]
DIRS = [(dz, dy) for dz in (-1, 0, 1) for dy in (-1, 0, 1) if (dz, dy) != (0, 0)]


def over(count, body):
    if count <= 16:
        for i in range(1, count):
            body(i)
    else:
        lax.fori_loop(1, count, lambda i, c: (body(i), c)[1], 0)


def solve4(m, g):
    m = [list(row) for row in m]
    g = list(g)
    inv = [None] * 4
    for k in range(4):
        inv[k] = 1.0 / m[k][k]
        for i in range(k + 1, 4):
            fac = m[i][k] * inv[k]
            for j in range(k + 1, i + 1):
                m[i][j] = m[i][j] - fac * m[j][k]
            g[i] = g[i] - fac * g[k]
    c = [None] * 4
    for k in range(3, -1, -1):
        value = g[k]
        for i in range(k + 1, 4):
            value = value - m[i][k] * c[i]
        c[k] = value * inv[k]
    return c


def coefficients(total):
    full = jnp.broadcast_to(jnp.sum(total, axis=1, keepdims=True), total.shape)
    gram = {}
    for at, (i, j) in enumerate(PAIRS):
        gram[i, j] = gram[j, i] = full[at : at + 1, :]
    m = [
        [
            3.5 * ((gram[i, j + 1] + gram[i, j]) + (gram[j, i + 1] + gram[j, i]))
            if j <= i
            else None
            for j in range(4)
        ]
        for i in range(4)
    ]
    return solve4(m, [gram[i, 0] for i in range(4)])


def kernel(
    n_slab, n_tile, rs, diag, index, order, conduct, level,
    sol, res, flow,
    ext, basis, ext2, basis2, dm, wt, first, msg1, part1, sum1, all1, msg2, part2, sum2, all2,
    h1s, h1r, h2s, h2r, a1s, a1r, b1s, b1r, a2s, a2r, b2s, b2r,
):
    cz, cy, nx = rs.shape
    plates, inlets = index.shape[2], index.shape[3]
    per = conduct.shape[0]
    me_s, me_t = lax.axis_index("slab"), lax.axis_index("tile")
    z_all, y_all = cz + 2 * HALO, cy + 2 * PAD
    own_z, own_y = slice(HALO, HALO + cz), slice(PAD, PAD + cy)

    ext[...] = jnp.zeros_like(ext)
    ext2[...] = jnp.zeros_like(ext2)
    ext[0, own_z, own_y, :] = rs[...]
    ext[1, own_z, own_y, :] = diag[...]

    barrier = pltpu.get_barrier_semaphore()

    def there(dz, dy):
        s, t = me_s + dz, me_t + dy
        return s, t, (s >= 0) & (s < n_slab) & (t >= 0) & (t < n_tile)

    for dz, dy in DIRS:
        if dz and dy:
            s, t, ok = there(dz, dy)

            @pl.when(ok)
            def _():
                pl.semaphore_signal(barrier, inc=1, device_id=(s, t), device_id_type=MESH)

    over(n_tile, lambda i: pl.semaphore_signal(
        barrier, inc=1, device_id=(me_s, lax.rem(me_t + i, n_tile)), device_id_type=MESH))
    over(n_slab, lambda i: pl.semaphore_signal(
        barrier, inc=1, device_id=(lax.rem(me_s + i, n_slab), me_t), device_id_type=MESH))
    beside_s = jnp.where(me_s > 0, 1, 0) + jnp.where(me_s < n_slab - 1, 1, 0)
    beside_t = jnp.where(me_t > 0, 1, 0) + jnp.where(me_t < n_tile - 1, 1, 0)
    pl.semaphore_wait(barrier, beside_s * beside_t + (n_tile - 1 + n_slab - 1))

    def halo_copy(ref, lead, at, send, recv):
        dz, dy = DIRS[at]
        src_z = {-1: slice(HALO, 2 * HALO), 0: own_z, 1: slice(cz, cz + HALO)}[dz]
        dst_z = {-1: slice(HALO + cz, z_all), 0: own_z, 1: slice(0, HALO)}[dz]
        src_y = {
            -1: slice(PAD, PAD + HALO), 0: own_y, 1: slice(PAD + cy - HALO, PAD + cy)
        }[dy]
        dst_y = {
            -1: slice(PAD + cy, PAD + cy + HALO), 0: own_y, 1: slice(PAD - HALO, PAD)
        }[dy]
        cut = lambda z, y: ref.at[lead + (pl.ds(z.start, z.stop - z.start), pl.ds(y.start, y.stop - y.start))]
        return pltpu.make_async_remote_copy(
            src_ref=cut(src_z, src_y), dst_ref=cut(dst_z, dst_y),
            send_sem=send.at[at], recv_sem=recv.at[at],
            device_id=(me_s + dz, me_t + dy), device_id_type=MESH,
        )

    def halo_start(ref, lead, send, recv):
        for at, (dz, dy) in enumerate(DIRS):

            @pl.when(there(dz, dy)[2])
            def _():
                halo_copy(ref, lead, at, send, recv).start()

    def halo_recv(ref, lead, send, recv):
        for at, (dz, dy) in enumerate(DIRS):

            @pl.when(there(-dz, -dy)[2])
            def _():
                halo_copy(ref, lead, at, send, recv).wait_recv()

    def halo_sent(ref, lead, send, recv):
        for at, (dz, dy) in enumerate(DIRS):

            @pl.when(there(dz, dy)[2])
            def _():
                halo_copy(ref, lead, at, send, recv).wait_send()

    halo_start(ext, (slice(None),), h1s, h1r)

    cells = index[0, 0]
    lanes = lax.broadcasted_iota(jnp.int32, (plates, nx), 1)
    hot = []
    for slot in range(inlets):
        where = jnp.broadcast_to(cells[:, slot : slot + 1], (plates, nx))
        line = jnp.where(where // nx == lanes, 1.0, 0.0).astype(jnp.bfloat16)
        hot.append(line)
    for slot in range(inlets):
        first[slot, :, 0:nx] = hot[slot]
        first[slot, :, nx:2 * nx] = hot[slot]

    for z in range(z_all):
        gz = me_s * cz + (z - HALO)
        gy = me_t * cy - PAD + lax.broadcasted_iota(jnp.int32, (y_all, nx), 0)
        inside = (gy >= 0) & (gy < n_tile * cy) & (gz >= 0) & (gz < n_slab * cz)
        wt[z] = jnp.where(inside, 1.0 / 7.0, 0.0)

    halo_recv(ext, (slice(None),), h1s, h1r)
    for z in range(z_all):
        dm[z] = (ext[1, z] - 1.0) * (1.0 / 7.0)

    lane_at = lax.broadcasted_iota(jnp.int32, (y_all, nx), 1)

    def powers(read, store):
        for k in range(STEPS):
            for z in range(k + 1, z_all - 1 - k):
                c = read(k, z)
                beside = read(k, z + 1) + read(k, z - 1)
                beside = beside + (pltpu.roll(c, 1, 0) + pltpu.roll(c, y_all - 1, 0))
                beside = beside + (
                    jnp.where(lane_at == 0, 0.0, pltpu.roll(c, 1, 1))
                    + jnp.where(lane_at == nx - 1, 0.0, pltpu.roll(c, nx - 1, 1))
                )
                store[k, z] = dm[z] * c - wt[z] * beside

    def products(own, msg):
        acc = [None] * len(PAIRS)
        for z in range(HALO, HALO + cz):
            v = [own(k, z) for k in range(5)]
            for at, (i, j) in enumerate(PAIRS):
                term = v[i] * v[j]
                acc[at] = term if acc[at] is None else acc[at] + term
        for at in range(len(PAIRS)):
            msg[at : at + 1, :] = jnp.sum(acc[at], axis=0, keepdims=True)
        msg[15:16, :] = jnp.zeros((1, nx), jnp.float32)

    def exchange(axis_at, count, msg, slots, send, recv):
        me = (me_s, me_t)[axis_at]

        def place(i):
            return lax.rem(me + i, count)

        def copy(to, slot):
            return pltpu.make_async_remote_copy(
                src_ref=msg, dst_ref=slots.at[slot],
                send_sem=send.at[to], recv_sem=recv.at[slot],
                device_id=(to, me_t) if axis_at == 0 else (me_s, to), device_id_type=MESH,
            )

        over(count, lambda i: copy(place(i), me).start())
        slots[me] = msg[...]
        over(count, lambda i: copy(place(i), place(i)).wait_recv())

        def sent():
            over(count, lambda i: copy(place(i), place(i)).wait_send())

        return sent

    def added(count, slots):
        if count <= 16:
            total = slots[0]
            for i in range(1, count):
                total = total + slots[i]
            return total
        return lax.fori_loop(1, count, lambda i, t: t + slots[i], slots[0])

    def read1(k, z):
        return ext[0, z] if k == 0 else basis[k - 1, z]

    def own1(k, z):
        return ext[0, z, own_y, :] if k == 0 else basis[k - 1, z, own_y, :]

    powers(read1, basis)
    products(own1, msg1)
    sent1 = exchange(1, n_tile, msg1, part1, a1s, a1r)
    sum1[...] = added(n_tile, part1)
    sent2 = exchange(0, n_slab, sum1, all1, b1s, b1r)
    c1 = coefficients(added(n_slab, all1))
    keep = [1.0 - 7.0 * c1[0]] + [-7.0 * (c1[k] + c1[k - 1]) for k in (1, 2, 3)] + [-7.0 * c1[3]]
    for z in range(HALO, HALO + cz):
        v = [own1(k, z) for k in range(5)]
        x = c1[0] * v[0]
        r = v[0]
        for k in range(4):
            if k:
                x = x + c1[k] * v[k]
            r = r - (7.0 * c1[k]) * (v[k + 1] + v[k])
        sol[z - HALO] = x
        ext2[z, own_y, :] = r
    halo_start(ext2, (), h2s, h2r)
    sent1()
    sent2()
    halo_sent(ext, (slice(None),), h1s, h1r)
    halo_recv(ext2, (), h2s, h2r)

    def read2(k, z):
        return ext2[z] if k == 0 else basis2[k - 1, z]

    def own2(k, z):
        return ext2[z, own_y, :] if k == 0 else basis2[k - 1, z, own_y, :]

    powers(read2, basis2)
    products(own2, msg2)

    fields = [jnp.concatenate([sol[z] for z in range(cz)], axis=0)] + [
        jnp.concatenate([own2(k, z) for z in range(HALO, HALO + cz)], axis=0) for k in range(4)
    ]
    table = jnp.zeros((plates, nx), jnp.float32)
    for at, field in enumerate(fields):
        high = field.astype(jnp.bfloat16)
        low = (field - high.astype(jnp.float32)).astype(jnp.bfloat16)
        both = jnp.concatenate([high, low], axis=0)
        total = None
        for slot in range(inlets):
            got = jnp.dot(first[slot], both, preferred_element_type=jnp.float32)
            where = jnp.broadcast_to(cells[:, slot : slot + 1], (plates, nx))
            got = jnp.where(where % nx == lanes, got, 0.0)
            total = got if total is None else total + got
        table = jnp.where(lanes == at, jnp.sum(total, axis=1, keepdims=True), table)
    msg2[16:, :] = table

    sent3 = exchange(1, n_tile, msg2, part2, a2s, a2r)
    sum2[...] = added(n_tile, part2)
    sent4 = exchange(0, n_slab, sum2, all2, b2s, b2r)
    everything = added(n_slab, all2)
    c2 = coefficients(everything[:16])
    for z in range(HALO, HALO + cz):
        v = [own2(k, z) for k in range(5)]
        x = sol[z - HALO]
        r = v[0]
        for k in range(4):
            x = x + c2[k] * v[k]
            r = r - (7.0 * c2[k]) * (v[k + 1] + v[k])
        sol[z - HALO] = x
        res[z - HALO] = r

    lane1 = lax.broadcasted_iota(jnp.int32, (1, nx), 1)
    mix = jnp.where(lane1 == 0, 1.0, 0.0)
    for k in range(4):
        mix = jnp.where(lane1 == k + 1, c2[k], mix)
    contrib = jnp.sum(everything[16:] * mix, axis=1, keepdims=True)
    contrib = jnp.broadcast_to(contrib, (plates, nx))
    plate_at = lax.broadcasted_iota(jnp.int32, (plates, nx), 0)
    scale = 1.0 / (float(n_slab * n_tile * inlets) ** 0.5)
    row = jnp.zeros((1, nx), jnp.float32)
    for j in range(per):
        spot = me_t * per + j
        header = jnp.sum(
            jnp.where(plate_at == order[spot], contrib, 0.0), axis=0, keepdims=True
        )
        row = jnp.where(lane1 == j, conduct[j] * (header * scale - level[j]), row)
    flow[...] = row[:, :per]

    sent3()
    sent4()
    halo_sent(ext2, (), h2s, h2r)


def on_device(n_slab, n_tile, right_side, diagonal, inlet_index, plate_order, conductance, plate_level):
    cz, cy, nx = right_side.shape
    plates, inlets = inlet_index.shape[2:]
    per = conductance.shape[0]
    z_all, y_all = cz + 2 * HALO, cy + 2 * PAD
    f32 = jnp.float32
    block = jax.ShapeDtypeStruct((cz, cy, nx), f32)
    vmem = pl.BlockSpec(memory_space=pltpu.VMEM)
    smem = pl.BlockSpec(memory_space=pltpu.SMEM)
    rows2 = 16 + plates
    dma = pltpu.SemaphoreType.DMA
    sol, res, flow = pl.pallas_call(
        functools.partial(kernel, n_slab, n_tile),
        out_shape=(block, block, jax.ShapeDtypeStruct((1, per), f32)),
        in_specs=[vmem, vmem, vmem, smem, smem, smem],
        out_specs=(vmem, vmem, vmem),
        scratch_shapes=[
            pltpu.VMEM((2, z_all, y_all, nx), f32),
            pltpu.VMEM((4, z_all, y_all, nx), f32),
            pltpu.VMEM((z_all, y_all, nx), f32),
            pltpu.VMEM((4, z_all, y_all, nx), f32),
            pltpu.VMEM((z_all, y_all, nx), f32),
            pltpu.VMEM((z_all, y_all, nx), f32),
            pltpu.VMEM((inlets, plates, 2 * nx), jnp.bfloat16),
            pltpu.VMEM((16, nx), f32),
            pltpu.VMEM((n_tile, 16, nx), f32),
            pltpu.VMEM((16, nx), f32),
            pltpu.VMEM((n_slab, 16, nx), f32),
            pltpu.VMEM((rows2, nx), f32),
            pltpu.VMEM((n_tile, rows2, nx), f32),
            pltpu.VMEM((rows2, nx), f32),
            pltpu.VMEM((n_slab, rows2, nx), f32),
            dma((8,)), dma((8,)), dma((8,)), dma((8,)),
            dma((n_tile,)), dma((n_tile,)), dma((n_slab,)), dma((n_slab,)),
            dma((n_tile,)), dma((n_tile,)), dma((n_slab,)), dma((n_slab,)),
        ],
        compiler_params=pltpu.CompilerParams(
            collective_id=0, has_side_effects=True, vmem_limit_bytes=48 * 1024 * 1024
        ),
    )(right_side, diagonal, inlet_index, plate_order, conductance, plate_level)
    return sol, res, flow.reshape(per)


def solution(mesh):
    in_specs = (
        P("slab", "tile", None),
        P("slab", "tile", None),
        P("slab", "tile", None, None),
        P(),
        P("tile"),
        P("tile"),
    )
    out_specs = (P("slab", "tile", None), P("slab", "tile", None), P("tile"))
    return jax.shard_map(
        functools.partial(on_device, mesh.shape["slab"], mesh.shape["tile"]),
        mesh=mesh, in_specs=in_specs, out_specs=out_specs, check_vma=False,
    )
```

time: 325 us -> 36.7 us (0.11)
  blocking collectives: 137 us -> 0 us
  starting transfers between devices: 92.4 us -> 0 us
  Pallas kernels: 0 us -> 31.6 us
  local copies, waits for them, and re-layouts: 31.1 us -> 4.25 us
  between operations: 27.5 us -> 0.68 us
  waiting for transfers between devices: 18.1 us -> 0 us
  other arithmetic: 14.1 us -> 0 us
    psum x3 -> x0, blocking collectives: 137 us -> none  [the longest x2 96.3 us: on_device(): gram_vec = lax.psum(local_gram, ('slab', 'tile'))]
    ppermute x32 -> x0, starting transfers between devices: 92.4 us -> none  [the longest x16 71.7 us: extended(): lax.ppermute(lax.slice_in_dim(block, block.shape[dim] - width, None, axis...]
    pallas_call x0 -> x1, Pallas kernels: none -> 31.6 us  [on_device(): pl.pallas_call(functools.partial(kernel, n_slab, n_tile), out_shape=(bloc...]
    another operation x4 -> x0, local copies, waits for them, and re-layouts: 19.5 us -> none  [the longest x2 19 us: local_products(): return jnp.stack([full[pair[0], pair[1]] for pair in GRAM_PAIRS])]
    ppermute x32 -> x0, waiting for transfers between devices: 18.1 us -> none  [the longest x16 15.2 us: extended(): lax.ppermute(lax.slice_in_dim(block, block.shape[dim] - width, None, axis...]
    another operation x14 -> x0, other arithmetic: 10.3 us -> none  [the longest x7 8.13 us: solve_block(): jnp.stack([jnp.stack([entries[row_at, col_at] for col_at in range(5)]) fo...]
    slice x29 -> x0, local copies, waits for them, and re-layouts: 5.97 us -> none  [the longest x2 1.46 us: local_products(): return jnp.stack([full[pair[0], pair[1]] for pair in GRAM_PAIRS])]
    gather x3 -> x0, local copies, waits for them, and re-layouts: 3.93 us -> none  [the longest x2 3.22 us: on_device(): picked = jnp.take(flat_field, inlet_index[0, 0], axis=0)]
  transfers between devices with their start and end apart: 32 -> 0, of which waited for: 16 -> 0; matrix products, arithmetic and copies ran while one was open for 1% -> 0% of each run, Pallas kernels for 0% -> 0%
where the time goes in v1:
time: 36.7 us; the launch traced here: 36.5 us
  Pallas kernels  31.6 us (86%)
  local copies, waits for them, and re-layouts  4.25 us (12%)
  between operations  0.68 us (2%)
    pallas_call x1, Pallas kernels, on_device(): pl.pallas_call(functools.partial(kernel, n_slab, n_tile), out_shape=(bloc...  31.6 us
    unnamed x14, local copies, waits for them, and re-layouts  4.25 us

profile of v1, /device:TPU:0, one launch (start us, length us, event | category | flops | bytes accessed | tf_op | source)
XLA Modules:
  0.0 36.5 jit_solution(12737238312625993632)
XLA Ops:
  0.6 0.0 copy-start.4
  0.6 0.0 copy-start.3
  0.7 0.0 copy-start.2
  0.7 0.8 %copy.9.index = s32[1,1,32,16]{3,2,1,0:T(8,128)S(1)} copy(s32[1,1,32,16]{2,3,1,0:T(8,128)} %param.8) | data formatting | bytes 4096 | tf_op args[2]
  1.4 0.0 copy-done.4
  1.5 0.0 copy-done.3
  1.5 0.0 copy-done.2
  1.5 0.0 copy-start
  1.5 0.8 %copy-done = f32[8,16,128]{2,1,0:T(8,128)S(1)} copy-done((f32[8,16,128]{2,1,0:T(8,128)S(1)}, f32[8,16,128]{2,1,0:T(8,128)}, u32[]{:S(2)}) %copy-start) | copy-done | bytes 65560
  2.3 0.0 copy-start.1
  2.3 0.8 %copy-done.1 = f32[8,16,128]{2,1,0:T(8,128)S(1)} copy-done((f32[8,16,128]{2,1,0:T(8,128)S(1)}, f32[8,16,128]{2,1,0:T(8,128)}, u32[]{:S(2)}) %copy-start.1) | copy-done | bytes 65560
  3.1 31.6 %shard_map.85 = (f32[8,16,128]{2,1,0:T(8,128)S(1)}, f32[8,16,128]{2,1,0:T(8,128)S(1)}, f32[1,4]{1,0:T(1,128)S(1)}) custom-call(f32[8,16,128]{2,1,0:T(8,128)S(1)} %copy-done, f32[8,16,128]{2,1,0:T(8,128)S(1)} %copy-done.1, s32[1,1,32,16]{3,2,1,0:T(8,128)S(1)} %copy.9.index, s32[32]{0:T(128)S(1)} %copy-done.2, f32[4]{0:T(128)S(1)} %copy-done.3, f32[4]{0:T(128)S(1)} %copy-done.4), custom_call_target="tpu_custom_call" | custom-call | tf_op jit(solution)/shard_map/pallas_call | solution.py:322
  34.7 0.6 %copy.13 = f32[8,16,128]{2,1,0:T(8,128)} copy(f32[8,16,128]{2,1,0:T(8,128)S(1)} %get-tuple-element.12) | data formatting | bytes 131072
  35.3 0.6 %copy.14 = f32[8,16,128]{2,1,0:T(8,128)} copy(f32[8,16,128]{2,1,0:T(8,128)S(1)} %get-tuple-element.13) | data formatting | bytes 131072
  36.0 0.5 %copy.15 = f32[4]{0:T(128)} copy(f32[4]{0:T(128)S(1)} %bitcast.1) | data formatting | bytes 32
Async XLA Ops:
  0.6 0.8 %copy-start.4 = (f32[4]{0:T(128)S(1)}, f32[4]{0:T(128)}, u32[]{:S(2)}) copy-start(f32[4]{0:T(128)} %level.1) | copy-start | bytes 52
  0.6 0.8 %copy-start.3 = (f32[4]{0:T(128)S(1)}, f32[4]{0:T(128)}, u32[]{:S(2)}) copy-start(f32[4]{0:T(128)} %conduct.1) | copy-start | bytes 52
  0.7 0.8 %copy-start.2 = (s32[32]{0:T(128)S(1)}, s32[32]{0:T(128)}, u32[]{:S(2)}) copy-start(s32[32]{0:T(128)} %order.1) | copy-start | bytes 388
  1.5 0.8 %copy-start = (f32[8,16,128]{2,1,0:T(8,128)S(1)}, f32[8,16,128]{2,1,0:T(8,128)}, u32[]{:S(2)}) copy-start(f32[8,16,128]{2,1,0:T(8,128)} %rs.1) | copy-start | bytes 196612
  2.3 0.8 %copy-start.1 = (f32[8,16,128]{2,1,0:T(8,128)S(1)}, f32[8,16,128]{2,1,0:T(8,128)}, u32[]{:S(2)}) copy-start(f32[8,16,128]{2,1,0:T(8,128)} %diag.1) | copy-start | bytes 196612

commit v2 on v1

v2 whole, which is shorter than its diff:
```python
import functools

import jax
import jax.numpy as jnp
from jax import lax
from jax.experimental import pallas as pl
from jax.experimental.pallas import tpu as pltpu
from jax.sharding import PartitionSpec as P

STEPS = 4
HALO = 4
PAD = 8
MESH = pl.DeviceIdType.MESH
PAIRS = [(i, j) for i in range(5) for j in range(i, 5)]
ANY = pl.BlockSpec(memory_space=pl.ANY)
VMEM = pl.BlockSpec(memory_space=pltpu.VMEM)
DIRS = [(dz, dy) for dz in (-1, 0, 1) for dy in (-1, 0, 1) if (dz, dy) != (0, 0)]


def over(count, body):
    if count <= 32:
        for i in range(1, count):
            body(i)
    else:
        lax.fori_loop(1, count, lambda i, c: (body(i), c)[1], 0)


def solve4(m, g):
    m = [list(row) for row in m]
    g = list(g)
    inv = [None] * 4
    for k in range(4):
        inv[k] = 1.0 / m[k][k]
        for i in range(k + 1, 4):
            fac = m[i][k] * inv[k]
            for j in range(k + 1, i + 1):
                m[i][j] = m[i][j] - fac * m[j][k]
            g[i] = g[i] - fac * g[k]
    c = [None] * 4
    for k in range(3, -1, -1):
        value = g[k]
        for i in range(k + 1, 4):
            value = value - m[i][k] * c[i]
        c[k] = value * inv[k]
    return c


def to_lanes(column, at):
    sub = lax.broadcasted_iota(jnp.int32, column.shape, 0)
    lane = lax.broadcasted_iota(jnp.int32, column.shape, 1)
    return jnp.sum(jnp.where(lane + at == sub, column, 0.0), axis=0, keepdims=True)


def coefficients(row):
    sub = lax.broadcasted_iota(jnp.int32, (16, row.shape[1]), 0)
    lane = lax.broadcasted_iota(jnp.int32, (16, row.shape[1]), 1)
    full = jnp.sum(jnp.where(lane == sub, row, 0.0), axis=1, keepdims=True)
    full = jnp.broadcast_to(full, sub.shape)
    gram = {}
    for at, (i, j) in enumerate(PAIRS):
        gram[i, j] = gram[j, i] = full[at : at + 1, :]
    m = [
        [
            3.5 * ((gram[i, j + 1] + gram[i, j]) + (gram[j, i + 1] + gram[j, i]))
            if j <= i
            else None
            for j in range(4)
        ]
        for i in range(4)
    ]
    return solve4(m, [gram[i, 0] for i in range(4)])


def kernel(
    n_slab, n_tile, rs, diag, index, order_in, conduct_in, level_in,
    sol, res, flow,
    ext, basis, ext2, basis2, dm, wt, cells, first, here,
    order, conduct, level, msg1, part1, msg2, part2, msg3, part3,
    h1s, h1r, h2s, h2r, a1s, a1r, a2s, a2r, a3s, a3r, local,
):
    cz, cy, nx = rs.shape
    inlets, plates = index.shape[2], index.shape[3]
    per = conduct.shape[0]
    me_s, me_t = lax.axis_index("slab"), lax.axis_index("tile")
    count, me = n_slab * n_tile, me_s * n_tile + me_t
    z_all, y_all = cz + 2 * HALO, cy + 2 * PAD
    own_z, own_y = slice(HALO, HALO + cz), slice(PAD, PAD + cy)

    own = lambda lead: ext.at[lead, pl.ds(HALO, cz), pl.ds(PAD, cy)]
    loads = [
        pltpu.make_async_copy(src, dst, local.at[at])
        for at, (src, dst) in enumerate([
            (rs, own(0)), (diag, own(1)), (index.at[0, 0], cells),
            (order_in, order), (conduct_in, conduct), (level_in, level),
        ])
    ]
    ext[...] = jnp.zeros_like(ext)
    ext2[...] = jnp.zeros_like(ext2)
    for load in loads:
        load.start()

    barrier = pltpu.get_barrier_semaphore()

    def there(dz, dy):
        s, t = me_s + dz, me_t + dy
        return s, t, (s >= 0) & (s < n_slab) & (t >= 0) & (t < n_tile)

    def place(i):
        at = lax.rem(me + i, count)
        return at, (at // n_tile, lax.rem(at, n_tile))

    over(count, lambda i: pl.semaphore_signal(
        barrier, inc=1, device_id=place(i)[1], device_id_type=MESH))
    loads[0].wait()
    loads[1].wait()
    pl.semaphore_wait(barrier, count - 1)

    def halo_copy(ref, lead, at, send, recv):
        dz, dy = DIRS[at]
        src_z = {-1: slice(HALO, 2 * HALO), 0: own_z, 1: slice(cz, cz + HALO)}[dz]
        dst_z = {-1: slice(HALO + cz, z_all), 0: own_z, 1: slice(0, HALO)}[dz]
        src_y = {
            -1: slice(PAD, PAD + HALO), 0: own_y, 1: slice(PAD + cy - HALO, PAD + cy)
        }[dy]
        dst_y = {
            -1: slice(PAD + cy, PAD + cy + HALO), 0: own_y, 1: slice(PAD - HALO, PAD)
        }[dy]
        cut = lambda z, y: ref.at[lead + (pl.ds(z.start, z.stop - z.start), pl.ds(y.start, y.stop - y.start))]
        return pltpu.make_async_remote_copy(
            src_ref=cut(src_z, src_y), dst_ref=cut(dst_z, dst_y),
            send_sem=send.at[at], recv_sem=recv.at[at],
            device_id=(me_s + dz, me_t + dy), device_id_type=MESH,
        )

    def halo_start(ref, lead, send, recv):
        for at, (dz, dy) in enumerate(DIRS):

            @pl.when(there(dz, dy)[2])
            def _():
                halo_copy(ref, lead, at, send, recv).start()

    def halo_recv(ref, lead, send, recv):
        for at, (dz, dy) in enumerate(DIRS):

            @pl.when(there(-dz, -dy)[2])
            def _():
                halo_copy(ref, lead, at, send, recv).wait_recv()

    def halo_sent(ref, lead, send, recv):
        for at, (dz, dy) in enumerate(DIRS):

            @pl.when(there(dz, dy)[2])
            def _():
                halo_copy(ref, lead, at, send, recv).wait_send()

    halo_start(ext, (slice(None),), h1s, h1r)

    loads[2].wait()
    lanes = lax.broadcasted_iota(jnp.int32, (plates, nx), 1)
    padded = jnp.concatenate(
        [cells[...], jnp.zeros((nx - inlets, plates), jnp.int32)], axis=0
    )
    if plates % nx:
        padded = jnp.concatenate(
            [padded, jnp.zeros((nx, nx - plates % nx), jnp.int32)], axis=1
        )
    spots = jnp.concatenate(
        [padded[:, at : at + nx].T for at in range(0, padded.shape[1], nx)], axis=0
    )[:plates]
    for slot in range(inlets):
        where = jnp.broadcast_to(spots[:, slot : slot + 1], (plates, nx))
        line = jnp.where(where // nx == lanes, 1.0, 0.0).astype(jnp.bfloat16)
        first[slot] = jnp.concatenate([line, line], axis=1)
        here[slot] = jnp.where(where % nx == lanes, 1.0, 0.0)

    for z in range(z_all):
        gz = me_s * cz + (z - HALO)
        gy = me_t * cy - PAD + lax.broadcasted_iota(jnp.int32, (y_all, nx), 0)
        inside = (gy >= 0) & (gy < n_tile * cy) & (gz >= 0) & (gz < n_slab * cz)
        wt[z] = jnp.where(inside, 1.0 / 7.0, 0.0)

    halo_recv(ext, (slice(None),), h1s, h1r)
    for z in range(z_all):
        dm[z] = (ext[1, z] - 1.0) * (1.0 / 7.0)

    lane_at = lax.broadcasted_iota(jnp.int32, (y_all, nx), 1)

    def powers(read, store):
        for k in range(STEPS):
            for z in range(k + 1, z_all - 1 - k):
                c = read(k, z)
                beside = read(k, z + 1) + read(k, z - 1)
                beside = beside + (pltpu.roll(c, 1, 0) + pltpu.roll(c, y_all - 1, 0))
                beside = beside + (
                    jnp.where(lane_at == 0, 0.0, pltpu.roll(c, 1, 1))
                    + jnp.where(lane_at == nx - 1, 0.0, pltpu.roll(c, nx - 1, 1))
                )
                store[k, z] = dm[z] * c - wt[z] * beside

    def products(own, msg):
        acc = [None] * len(PAIRS)
        for z in range(HALO, HALO + cz):
            v = [own(k, z) for k in range(5)]
            for at, (i, j) in enumerate(PAIRS):
                term = v[i] * v[j]
                acc[at] = term if acc[at] is None else acc[at] + term
        rows = [jnp.sum(term, axis=0, keepdims=True) for term in acc]
        rows = jnp.concatenate(rows + [jnp.zeros((1, nx), jnp.float32)], axis=0)
        column = jnp.broadcast_to(jnp.sum(rows, axis=1, keepdims=True), rows.shape)
        msg[0:1, :] = to_lanes(column, 0)

    def inlet_sums(fields):
        halves = []
        for field in fields:
            high = field.astype(jnp.bfloat16)
            low = (field - high.astype(jnp.float32)).astype(jnp.bfloat16)
            halves.append(jnp.concatenate([high, low], axis=0))
        got = jnp.dot(
            first[...].reshape(inlets * plates, 2 * nx),
            jnp.concatenate(halves, axis=1),
            preferred_element_type=jnp.float32,
        )
        sums = []
        for at in range(len(fields)):
            total = None
            for slot in range(inlets):
                term = here[slot] * got[
                    slot * plates : (slot + 1) * plates, at * nx : (at + 1) * nx
                ]
                total = term if total is None else total + term
            total = jnp.sum(total, axis=1, keepdims=True)
            sums.append(jnp.broadcast_to(total, (plates, nx)))
        return sums

    def send(msg, slots, rows, send_sem, recv_sem):
        def copy(i):
            return pltpu.make_async_remote_copy(
                src_ref=msg.at[pl.ds(0, rows)], dst_ref=slots.at[me, pl.ds(0, rows)],
                send_sem=send_sem, recv_sem=recv_sem,
                device_id=place(i)[1], device_id_type=MESH,
            )

        others = slots.at[pl.ds(0, count - 1), pl.ds(0, rows)]
        every = pltpu.make_async_remote_copy(
            src_ref=others, dst_ref=others, send_sem=send_sem, recv_sem=recv_sem,
            device_id=place(1)[1], device_id_type=MESH,
        )
        over(count, lambda i: copy(i).start())
        slots[me, 0:rows, :] = msg[0:rows, :]

        def total():
            every.wait_recv()
            if count <= 32:
                parts = [slots[i, 0:rows, :] for i in range(count)]
                while len(parts) > 1:
                    parts = [
                        parts[i] + parts[i + 1] if i + 1 < len(parts) else parts[i]
                        for i in range(0, len(parts), 2)
                    ]
                return parts[0]
            return lax.fori_loop(
                1, count, lambda i, t: t + slots[i, 0:rows, :], slots[0, 0:rows, :]
            )

        return total, every.wait_send

    def read1(k, z):
        return ext[0, z] if k == 0 else basis[k - 1, z]

    def own1(k, z):
        return ext[0, z, own_y, :] if k == 0 else basis[k - 1, z, own_y, :]

    powers(read1, basis)
    products(own1, msg1)
    total1, sent1 = send(msg1, part1, 1, a1s, a1r)
    whole = lambda own, k: jnp.concatenate(
        [own(k, z) for z in range(HALO, HALO + cz)], axis=0
    )
    picked1 = inlet_sums([whole(own1, k) for k in range(4)])
    c1 = coefficients(total1())
    for z in range(HALO, HALO + cz):
        v = [own1(k, z) for k in range(5)]
        x = c1[0] * v[0]
        r = v[0]
        for k in range(4):
            if k:
                x = x + c1[k] * v[k]
            r = r - (7.0 * c1[k]) * (v[k + 1] + v[k])
        sol[z - HALO] = x
        ext2[z, own_y, :] = r
    halo_start(ext2, (), h2s, h2r)
    sent1()
    halo_sent(ext, (slice(None),), h1s, h1r)
    halo_recv(ext2, (), h2s, h2r)

    def read2(k, z):
        return ext2[z] if k == 0 else basis2[k - 1, z]

    def own2(k, z):
        return ext2[z, own_y, :] if k == 0 else basis2[k - 1, z, own_y, :]

    powers(read2, basis2)
    products(own2, msg2)
    total2, sent2 = send(msg2, part2, 1, a2s, a2r)

    so_far = picked1[0] * c1[0]
    for k in range(1, 4):
        so_far = so_far + picked1[k] * c1[k]
    picked2 = inlet_sums([whole(own2, k) for k in range(4)])
    blocks = part3.shape[1] // 8
    for at in range(blocks):
        for row, column in enumerate([so_far] + picked2):
            msg3[at * 8 + row : at * 8 + row + 1, :] = to_lanes(column, at * nx)
        msg3[at * 8 + 5 : at * 8 + 8, :] = jnp.zeros((3, nx), jnp.float32)
    total3, sent3 = send(msg3, part3, 8 * blocks, a3s, a3r)

    c2 = coefficients(total2())
    for z in range(HALO, HALO + cz):
        v = [own2(k, z) for k in range(5)]
        x = sol[z - HALO]
        r = v[0]
        for k in range(4):
            x = x + c2[k] * v[k]
            r = r - (7.0 * c2[k]) * (v[k + 1] + v[k])
        sol[z - HALO] = x
        res[z - HALO] = r

    lane1 = lax.broadcasted_iota(jnp.int32, (1, nx), 1)
    scale = 1.0 / (float(count * inlets) ** 0.5)
    sums = total3()
    contrib = []
    for at in range(blocks):
        value = sums[at * 8 : at * 8 + 1, :]
        for k in range(4):
            value = value + c2[k] * sums[at * 8 + 1 + k : at * 8 + 2 + k, :]
        contrib.append(value)
    for load in loads[3:]:
        load.wait()
    row = jnp.zeros((1, nx), jnp.float32)
    for j in range(per):
        plate = order[me_t * per + j]
        header = jnp.zeros((1, nx), jnp.float32)
        for at in range(blocks):
            header = header + jnp.where(lane1 + at * nx == plate, contrib[at], 0.0)
        header = jnp.sum(header, axis=1, keepdims=True)
        row = jnp.where(lane1 == j, conduct[j] * (header * scale - level[j]), row)
    flow[...] = row[:, :per]

    sent2()
    sent3()
    halo_sent(ext2, (), h2s, h2r)


def deliver(sol, res, flow, sol_out, res_out, flow_out, sems):
    copies = [
        pltpu.make_async_copy(src, dst, sems.at[at])
        for at, (src, dst) in enumerate([(sol, sol_out), (res, res_out), (flow, flow_out)])
    ]
    for copy in copies:
        copy.start()
    for copy in copies:
        copy.wait()


def on_device(n_slab, n_tile, right_side, diagonal, inlet_index, plate_order, conductance, plate_level):
    cz, cy, nx = right_side.shape
    inlet_index = inlet_index.transpose(0, 1, 3, 2)
    inlets, plates = inlet_index.shape[2:]
    per = conductance.shape[0]
    z_all, y_all = cz + 2 * HALO, cy + 2 * PAD
    count = n_slab * n_tile
    rows3 = 8 * -(-plates // nx)
    f32, i32 = jnp.float32, jnp.int32
    block = jax.ShapeDtypeStruct((cz, cy, nx), f32)
    shapes = (block, block, jax.ShapeDtypeStruct((1, per), f32))
    dma = pltpu.SemaphoreType.DMA
    results = pl.pallas_call(
        functools.partial(kernel, n_slab, n_tile),
        out_shape=tuple(pltpu.VMEM(leaf.shape, leaf.dtype) for leaf in shapes),
        in_specs=[ANY] * 6,
        out_specs=(VMEM,) * 3,
        scratch_shapes=[
            pltpu.VMEM((2, z_all, y_all, nx), f32),
            pltpu.VMEM((4, z_all, y_all, nx), f32),
            pltpu.VMEM((z_all, y_all, nx), f32),
            pltpu.VMEM((4, z_all, y_all, nx), f32),
            pltpu.VMEM((z_all, y_all, nx), f32),
            pltpu.VMEM((z_all, y_all, nx), f32),
            pltpu.VMEM((inlets, plates), i32),
            pltpu.VMEM((inlets, plates, 2 * nx), jnp.bfloat16),
            pltpu.VMEM((inlets, plates, nx), f32),
            pltpu.SMEM(plate_order.shape, i32),
            pltpu.SMEM((per,), f32),
            pltpu.SMEM((per,), f32),
            pltpu.VMEM((8, nx), f32),
            pltpu.VMEM((count, 8, nx), f32),
            pltpu.VMEM((8, nx), f32),
            pltpu.VMEM((count, 8, nx), f32),
            pltpu.VMEM((rows3, nx), f32),
            pltpu.VMEM((count, rows3, nx), f32),
            dma((8,)), dma((8,)), dma((8,)), dma((8,)),
            dma, dma, dma, dma, dma, dma, dma((6,)),
        ],
        compiler_params=pltpu.CompilerParams(
            collective_id=0, has_side_effects=True, vmem_limit_bytes=60 * 1024 * 1024
        ),
    )(right_side, diagonal, inlet_index, plate_order, conductance, plate_level)
    sol, res, flow = pl.pallas_call(
        deliver,
        out_shape=shapes,
        in_specs=[VMEM] * 3,
        out_specs=(ANY,) * 3,
        scratch_shapes=[dma((3,))],
    )(*results)
    return sol, res, flow.reshape(per)


def solution(mesh):
    in_specs = (
        P("slab", "tile", None),
        P("slab", "tile", None),
        P("slab", "tile", None, None),
        P(),
        P("tile"),
        P("tile"),
    )
    out_specs = (P("slab", "tile", None), P("slab", "tile", None), P("tile"))
    return jax.shard_map(
        functools.partial(on_device, mesh.shape["slab"], mesh.shape["tile"]),
        mesh=mesh, in_specs=in_specs, out_specs=out_specs, check_vma=False,
    )
```

time: 36.7 us -> 31.1 us (0.85)
  Pallas kernels: 31.6 us -> 28.5 us
  local copies, waits for them, and re-layouts: 4.25 us -> 1.77 us
    pallas_call x1 -> x2, Pallas kernels: 31.6 us -> 28.5 us  [the longest x1 27 us: on_device(): pl.pallas_call(functools.partial(kernel, n_slab, n_tile), out_shape=tuple...]
    unnamed x14 -> x6, local copies, waits for them, and re-layouts: 4.25 us -> 1.77 us
where the time goes in v2:
time: 31.1 us; the launch traced here: 30.9 us
  Pallas kernels  28.5 us (92%)
  local copies, waits for them, and re-layouts  1.77 us (6%)
  between operations  0.65 us (2%)
    pallas_call x1, Pallas kernels, on_device(): pl.pallas_call(functools.partial(kernel, n_slab, n_tile), out_shape=tuple...  27 us
    unnamed x6, local copies, waits for them, and re-layouts  1.77 us
    pallas_call x1, Pallas kernels, on_device(): pl.pallas_call(deliver, out_shape=shapes, in_specs=[VMEM] * 3, out_specs=...  1.55 us

profile of v2, /device:TPU:0, one launch (start us, length us, event | category | flops | bytes accessed | tf_op | source)
XLA Modules:
  0.0 30.9 jit_solution(9682590773058150649)
XLA Ops:
  0.6 27.0 %shard_map.85 = (f32[8,16,128]{2,1,0:T(8,128)S(1)}, f32[8,16,128]{2,1,0:T(8,128)S(1)}, f32[1,4]{1,0:T(1,128)S(1)}) custom-call(f32[8,16,128]{2,1,0:T(8,128)} %rs.1, f32[8,16,128]{2,1,0:T(8,128)} %diag.1, s32[1,1,16,32]{3,2,1,0:T(8,128)} %bitcast.2, s32[32]{0:T(128)} %order_in.1, f32[4]{0:T(128)} %conduct_in.1, f32[4]{0:T(128)} %level_in.1), custom_call_target="tpu_custom_call" | custom-call | tf_op jit(solution)/shard_map/pallas_call | solution.py:377
  27.6 0.0 copy-start
  27.6 0.6 %copy-done = f32[8,16,128]{2,1,0:T(8,128)} copy-done((f32[8,16,128]{2,1,0:T(8,128)}, f32[8,16,128]{2,1,0:T(8,128)S(1)}, u32[]{:S(2)}) %copy-start) | copy-done | bytes 65560
  28.2 0.0 copy-start.1
  28.2 0.6 %copy-done.1 = f32[8,16,128]{2,1,0:T(8,128)} copy-done((f32[8,16,128]{2,1,0:T(8,128)}, f32[8,16,128]{2,1,0:T(8,128)S(1)}, u32[]{:S(2)}) %copy-start.1) | copy-done | bytes 65560
  28.8 0.0 copy-start.2
  28.8 0.5 %copy-done.2 = f32[1,4]{1,0:T(1,128)} copy-done((f32[1,4]{1,0:T(1,128)}, f32[1,4]{1,0:T(1,128)S(1)}, u32[]{:S(2)}) %copy-start.2) | copy-done | bytes 40
  29.4 1.5 %shard_map.86 = (f32[8,16,128]{2,1,0:T(8,128)}, f32[8,16,128]{2,1,0:T(8,128)}, f32[1,4]{1,0:T(1,128)}) custom-call(f32[8,16,128]{2,1,0:T(8,128)} %copy-done, f32[8,16,128]{2,1,0:T(8,128)} %copy-done.1, f32[1,4]{1,0:T(1,128)} %copy-done.2), custom_call_target="tpu_custom_call" | custom-call | tf_op jit(solution)/shard_map/pallas_call | solution.py:408
Async XLA Ops:
  27.6 0.6 %copy-start = (f32[8,16,128]{2,1,0:T(8,128)}, f32[8,16,128]{2,1,0:T(8,128)S(1)}, u32[]{:S(2)}) copy-start(f32[8,16,128]{2,1,0:T(8,128)S(1)} %get-tuple-element.9.sol) | copy-start | bytes 196612
  28.2 0.6 %copy-start.1 = (f32[8,16,128]{2,1,0:T(8,128)}, f32[8,16,128]{2,1,0:T(8,128)S(1)}, u32[]{:S(2)}) copy-start(f32[8,16,128]{2,1,0:T(8,128)S(1)} %get-tuple-element.10.res) | copy-start | bytes 196612
  28.8 0.5 %copy-start.2 = (f32[1,4]{1,0:T(1,128)}, f32[1,4]{1,0:T(1,128)S(1)}, u32[]{:S(2)}) copy-start(f32[1,4]{1,0:T(1,128)S(1)} %get-tuple-element.11.flow) | copy-start | bytes 52

commit v3 on v2

--- a/solution.py
+++ b/solution.py
@@ -15,14 +15,6 @@
 ANY = pl.BlockSpec(memory_space=pl.ANY)
 VMEM = pl.BlockSpec(memory_space=pltpu.VMEM)
 DIRS = [(dz, dy) for dz in (-1, 0, 1) for dy in (-1, 0, 1) if (dz, dy) != (0, 0)]
-
-
-def over(count, body):
-    if count <= 32:
-        for i in range(1, count):
-            body(i)
-    else:
-        lax.fori_loop(1, count, lambda i, c: (body(i), c)[1], 0)
 
 
 def solve4(m, g):
@@ -86,6 +78,15 @@
     z_all, y_all = cz + 2 * HALO, cy + 2 * PAD
     own_z, own_y = slice(HALO, HALO + cz), slice(PAD, PAD + cy)
 
+    def halo_cut(at):
+        dz, dy = DIRS[at]
+        wide = HALO - 1 if dz and dy else HALO
+        src_z = {-1: slice(HALO, HALO + wide), 0: own_z, 1: slice(HALO + cz - wide, HALO + cz)}[dz]
+        dst_z = {-1: slice(HALO + cz, HALO + cz + wide), 0: own_z, 1: slice(HALO - wide, HALO)}[dz]
+        src_y = {-1: slice(PAD, PAD + wide), 0: own_y, 1: slice(PAD + cy - wide, PAD + cy)}[dy]
+        dst_y = {-1: slice(PAD + cy, PAD + cy + wide), 0: own_y, 1: slice(PAD - wide, PAD)}[dy]
+        return (src_z, src_y), (dst_z, dst_y)
+
     own = lambda lead: ext.at[lead, pl.ds(HALO, cz), pl.ds(PAD, cy)]
     loads = [
         pltpu.make_async_copy(src, dst, local.at[at])
@@ -94,8 +95,6 @@
             (order_in, order), (conduct_in, conduct), (level_in, level),
         ])
     ]
-    ext[...] = jnp.zeros_like(ext)
-    ext2[...] = jnp.zeros_like(ext2)
     for load in loads:
         load.start()
 
@@ -107,27 +106,42 @@
 
     def place(i):
         at = lax.rem(me + i, count)
-        return at, (at // n_tile, lax.rem(at, n_tile))
-
-    over(count, lambda i: pl.semaphore_signal(
-        barrier, inc=1, device_id=place(i)[1], device_id_type=MESH))
+        return lax.div(at, n_tile), lax.rem(at, n_tile)
+
+    def every_other(body):
+        if count <= 32:
+            slabs = [lax.rem(me_s + i, n_slab) for i in range(n_slab)]
+            tiles = [lax.rem(me_t + i, n_tile) for i in range(n_tile)]
+            for j in range(n_tile):
+                for i in range(n_slab):
+                    if i or j:
+                        body((slabs[i], tiles[j]))
+        else:
+            lax.fori_loop(1, count, lambda i, c: (body(place(i)), c)[1], 0)
+
+    every_other(lambda device: pl.semaphore_signal(
+        barrier, inc=1, device_id=device, device_id_type=MESH))
+
+    for at, (dz, dy) in enumerate(DIRS):
+
+        @pl.when(jnp.logical_not(there(-dz, -dy)[2]))
+        def _():
+            z, y = halo_cut(at)[1]
+            ext[:, z, y, :] = jnp.zeros((2, z.stop - z.start, y.stop - y.start, nx), jnp.float32)
+            ext2[z, y, :] = jnp.zeros((z.stop - z.start, y.stop - y.start, nx), jnp.float32)
+
     loads[0].wait()
     loads[1].wait()
     pl.semaphore_wait(barrier, count - 1)
 
     def halo_copy(ref, lead, at, send, recv):
         dz, dy = DIRS[at]
-        src_z = {-1: slice(HALO, 2 * HALO), 0: own_z, 1: slice(cz, cz + HALO)}[dz]
-        dst_z = {-1: slice(HALO + cz, z_all), 0: own_z, 1: slice(0, HALO)}[dz]
-        src_y = {
-            -1: slice(PAD, PAD + HALO), 0: own_y, 1: slice(PAD + cy - HALO, PAD + cy)
-        }[dy]
-        dst_y = {
-            -1: slice(PAD + cy, PAD + cy + HALO), 0: own_y, 1: slice(PAD - HALO, PAD)
-        }[dy]
-        cut = lambda z, y: ref.at[lead + (pl.ds(z.start, z.stop - z.start), pl.ds(y.start, y.stop - y.start))]
+        src, dst = halo_cut(at)
+        cut = lambda z, y: ref.at[
+            lead + (pl.ds(z.start, z.stop - z.start), pl.ds(y.start, y.stop - y.start))
+        ]
         return pltpu.make_async_remote_copy(
-            src_ref=cut(src_z, src_y), dst_ref=cut(dst_z, dst_y),
+            src_ref=cut(*src), dst_ref=cut(*dst),
             send_sem=send.at[at], recv_sem=recv.at[at],
             device_id=(me_s + dz, me_t + dy), device_id_type=MESH,
         )
@@ -233,19 +247,19 @@
         return sums
 
     def send(msg, slots, rows, send_sem, recv_sem):
-        def copy(i):
+        def copy(device):
             return pltpu.make_async_remote_copy(
                 src_ref=msg.at[pl.ds(0, rows)], dst_ref=slots.at[me, pl.ds(0, rows)],
                 send_sem=send_sem, recv_sem=recv_sem,
-                device_id=place(i)[1], device_id_type=MESH,
+                device_id=device, device_id_type=MESH,
             )
 
         others = slots.at[pl.ds(0, count - 1), pl.ds(0, rows)]
         every = pltpu.make_async_remote_copy(
             src_ref=others, dst_ref=others, send_sem=send_sem, recv_sem=recv_sem,
-            device_id=place(1)[1], device_id_type=MESH,
+            device_id=place(1), device_id_type=MESH,
         )
-        over(count, lambda i: copy(i).start())
+        every_other(lambda device: copy(device).start())
         slots[me, 0:rows, :] = msg[0:rows, :]
 
         def total():
@@ -411,6 +425,7 @@
         in_specs=[VMEM] * 3,
         out_specs=(ANY,) * 3,
         scratch_shapes=[dma((3,))],
+        compiler_params=pltpu.CompilerParams(vmem_limit_bytes=1024 * 1024),
     )(*results)
     return sol, res, flow.reshape(per)
 

time: 31.1 us -> 27.6 us (0.89)
  local copies, waits for them, and re-layouts: 1.77 us -> 0 us
  Pallas kernels: 28.5 us -> 26.8 us
    unnamed x6 -> x0, local copies, waits for them, and re-layouts: 1.77 us -> none
    pallas_call x1, Pallas kernels: 1.55 us -> 0.68 us  [on_device(): pl.pallas_call(deliver, out_shape=shapes, in_specs=[VMEM] * 3, out_specs=...]
    pallas_call x1, Pallas kernels: 27 us -> 26.1 us  [on_device(): pl.pallas_call(functools.partial(kernel, n_slab, n_tile), out_shape=tuple...]
where the time goes in v3:
time: 27.6 us; the launch traced here: 27.5 us
  Pallas kernels  26.8 us (97%)
  between operations  0.64 us (2%)
    pallas_call x1, Pallas kernels, on_device(): pl.pallas_call(functools.partial(kernel, n_slab, n_tile), out_shape=tuple...  26.1 us
    pallas_call x1, Pallas kernels, on_device(): pl.pallas_call(deliver, out_shape=shapes, in_specs=[VMEM] * 3, out_specs=...  0.68 us

profile of v3, /device:TPU:0, one launch (start us, length us, event | category | flops | bytes accessed | tf_op | source)
XLA Modules:
  0.0 27.5 jit_solution(17137791278926577349)
XLA Ops:
  0.6 26.1 %shard_map.85 = (f32[8,16,128]{2,1,0:T(8,128)S(1)}, f32[8,16,128]{2,1,0:T(8,128)S(1)}, f32[1,4]{1,0:T(1,128)S(1)}) custom-call(f32[8,16,128]{2,1,0:T(8,128)} %rs.1, f32[8,16,128]{2,1,0:T(8,128)} %diag.1, s32[1,1,16,32]{3,2,1,0:T(8,128)} %bitcast.2, s32[32]{0:T(128)} %order_in.1, f32[4]{0:T(128)} %conduct_in.1, f32[4]{0:T(128)} %level_in.1), custom_call_target="tpu_custom_call" | custom-call | tf_op jit(solution)/shard_map/pallas_call | solution.py:391
  26.8 0.7 %shard_map.86 = (f32[8,16,128]{2,1,0:T(8,128)}, f32[8,16,128]{2,1,0:T(8,128)}, f32[1,4]{1,0:T(1,128)}) custom-call(f32[8,16,128]{2,1,0:T(8,128)S(1)} %get-tuple-element.9.sol, f32[8,16,128]{2,1,0:T(8,128)S(1)} %get-tuple-element.10.res, f32[1,4]{1,0:T(1,128)S(1)} %get-tuple-element.11.flow), custom_call_target="tpu_custom_call" | custom-call | tf_op jit(solution)/shard_map/pallas_call | solution.py:422

commit v4 on v3

--- a/solution.py
+++ b/solution.py
@@ -66,9 +66,9 @@
 def kernel(
     n_slab, n_tile, rs, diag, index, order_in, conduct_in, level_in,
     sol, res, flow,
-    ext, basis, ext2, basis2, dm, wt, cells, first, here,
-    order, conduct, level, msg1, part1, msg2, part2, msg3, part3,
-    h1s, h1r, h2s, h2r, a1s, a1r, a2s, a2r, a3s, a3r, local,
+    ext, basis, dm, wt, cells, first, here, coeffs,
+    order, conduct, level, msg1, part1, msg2, part2,
+    h1s, h1r, h2s, h2r, a1s, a1r, a2s, a2r, local,
 ):
     cz, cy, nx = rs.shape
     inlets, plates = index.shape[2], index.shape[3]
@@ -127,8 +127,7 @@
         @pl.when(jnp.logical_not(there(-dz, -dy)[2]))
         def _():
             z, y = halo_cut(at)[1]
-            ext[:, z, y, :] = jnp.zeros((2, z.stop - z.start, y.stop - y.start, nx), jnp.float32)
-            ext2[z, y, :] = jnp.zeros((z.stop - z.start, y.stop - y.start, nx), jnp.float32)
+            ext[:, z, y, :] = jnp.zeros((3, z.stop - z.start, y.stop - y.start, nx), jnp.float32)
 
     loads[0].wait()
     loads[1].wait()
@@ -167,7 +166,7 @@
             def _():
                 halo_copy(ref, lead, at, send, recv).wait_send()
 
-    halo_start(ext, (slice(None),), h1s, h1r)
+    halo_start(ext, (pl.ds(0, 2),), h1s, h1r)
 
     loads[2].wait()
     lanes = lax.broadcasted_iota(jnp.int32, (plates, nx), 1)
@@ -193,7 +192,7 @@
         inside = (gy >= 0) & (gy < n_tile * cy) & (gz >= 0) & (gz < n_slab * cz)
         wt[z] = jnp.where(inside, 1.0 / 7.0, 0.0)
 
-    halo_recv(ext, (slice(None),), h1s, h1r)
+    halo_recv(ext, (pl.ds(0, 2),), h1s, h1r)
     for z in range(z_all):
         dm[z] = (ext[1, z] - 1.0) * (1.0 / 7.0)
 
@@ -211,7 +210,7 @@
                 )
                 store[k, z] = dm[z] * c - wt[z] * beside
 
-    def products(own, msg):
+    def products(own):
         acc = [None] * len(PAIRS)
         for z in range(HALO, HALO + cz):
             v = [own(k, z) for k in range(5)]
@@ -221,7 +220,7 @@
         rows = [jnp.sum(term, axis=0, keepdims=True) for term in acc]
         rows = jnp.concatenate(rows + [jnp.zeros((1, nx), jnp.float32)], axis=0)
         column = jnp.broadcast_to(jnp.sum(rows, axis=1, keepdims=True), rows.shape)
-        msg[0:1, :] = to_lanes(column, 0)
+        return to_lanes(column, 0)
 
     def inlet_sums(fields):
         halves = []
@@ -246,26 +245,29 @@
             sums.append(jnp.broadcast_to(total, (plates, nx)))
         return sums
 
-    def send(msg, slots, rows, send_sem, recv_sem):
+    def send(msg, slots, at, rows, send_sem, recv_sem):
+        send_sem, recv_sem = send_sem.at[at], recv_sem.at[at]
+
         def copy(device):
             return pltpu.make_async_remote_copy(
-                src_ref=msg.at[pl.ds(0, rows)], dst_ref=slots.at[me, pl.ds(0, rows)],
+                src_ref=msg.at[at, pl.ds(0, rows)], dst_ref=slots.at[at, me, pl.ds(0, rows)],
                 send_sem=send_sem, recv_sem=recv_sem,
                 device_id=device, device_id_type=MESH,
             )
 
-        others = slots.at[pl.ds(0, count - 1), pl.ds(0, rows)]
+        others = slots.at[at, pl.ds(0, count - 1), pl.ds(0, rows)]
         every = pltpu.make_async_remote_copy(
             src_ref=others, dst_ref=others, send_sem=send_sem, recv_sem=recv_sem,
             device_id=place(1), device_id_type=MESH,
         )
-        every_other(lambda device: copy(device).start())
-        slots[me, 0:rows, :] = msg[0:rows, :]
+        def start():
+            every_other(lambda device: copy(device).start())
+            slots[at, me, 0:rows, :] = msg[at, 0:rows, :]
 
         def total():
             every.wait_recv()
             if count <= 32:
-                parts = [slots[i, 0:rows, :] for i in range(count)]
+                parts = [slots[at, i, 0:rows, :] for i in range(count)]
                 while len(parts) > 1:
                     parts = [
                         parts[i] + parts[i + 1] if i + 1 < len(parts) else parts[i]
@@ -273,81 +275,74 @@
                     ]
                 return parts[0]
             return lax.fori_loop(
-                1, count, lambda i, t: t + slots[i, 0:rows, :], slots[0, 0:rows, :]
+                1, count, lambda i, t: t + slots[at, i, 0:rows, :], slots[at, 0, 0:rows, :]
             )
 
-        return total, every.wait_send
-
-    def read1(k, z):
-        return ext[0, z] if k == 0 else basis[k - 1, z]
-
-    def own1(k, z):
-        return ext[0, z, own_y, :] if k == 0 else basis[k - 1, z, own_y, :]
-
-    powers(read1, basis)
-    products(own1, msg1)
-    total1, sent1 = send(msg1, part1, 1, a1s, a1r)
-    whole = lambda own, k: jnp.concatenate(
-        [own(k, z) for z in range(HALO, HALO + cz)], axis=0
-    )
-    picked1 = inlet_sums([whole(own1, k) for k in range(4)])
-    c1 = coefficients(total1())
-    for z in range(HALO, HALO + cz):
-        v = [own1(k, z) for k in range(5)]
-        x = c1[0] * v[0]
-        r = v[0]
+        return start, total, every.wait_send
+
+    blocks = -(-plates // nx)
+    grams = lambda at: send(msg1, part1, at, 1, a1s, a1r)
+    inlet = lambda at: send(msg2, part2, at, 4 * blocks, a2s, a2r)
+    sol[...] = jnp.zeros_like(sol)
+
+    def one_block(repeat, carry):
+        v0 = 2 * repeat
+
+        def read(k, z):
+            return ext[v0, z] if k == 0 else basis[k - 1, z]
+
+        def own(k, z):
+            return ext[v0, z, own_y, :] if k == 0 else basis[k - 1, z, own_y, :]
+
+        powers(read, basis)
+        msg1[repeat, 0:1, :] = products(own)
+        start, total, _ = grams(repeat)
+        start()
+
+        picked = inlet_sums([
+            jnp.concatenate([own(k, z) for z in range(HALO, HALO + cz)], axis=0)
+            for k in range(4)
+        ])
+        for k, column in enumerate(picked):
+            for at in range(blocks):
+                row = k * blocks + at
+                msg2[repeat, row : row + 1, :] = to_lanes(column, at * nx)
+        inlet(repeat)[0]()
+
+        c = coefficients(total())
         for k in range(4):
-            if k:
-                x = x + c1[k] * v[k]
-            r = r - (7.0 * c1[k]) * (v[k + 1] + v[k])
-        sol[z - HALO] = x
-        ext2[z, own_y, :] = r
-    halo_start(ext2, (), h2s, h2r)
-    sent1()
-    halo_sent(ext, (slice(None),), h1s, h1r)
-    halo_recv(ext2, (), h2s, h2r)
-
-    def read2(k, z):
-        return ext2[z] if k == 0 else basis2[k - 1, z]
-
-    def own2(k, z):
-        return ext2[z, own_y, :] if k == 0 else basis2[k - 1, z, own_y, :]
-
-    powers(read2, basis2)
-    products(own2, msg2)
-    total2, sent2 = send(msg2, part2, 1, a2s, a2r)
-
-    so_far = picked1[0] * c1[0]
-    for k in range(1, 4):
-        so_far = so_far + picked1[k] * c1[k]
-    picked2 = inlet_sums([whole(own2, k) for k in range(4)])
-    blocks = part3.shape[1] // 8
-    for at in range(blocks):
-        for row, column in enumerate([so_far] + picked2):
-            msg3[at * 8 + row : at * 8 + row + 1, :] = to_lanes(column, at * nx)
-        msg3[at * 8 + 5 : at * 8 + 8, :] = jnp.zeros((3, nx), jnp.float32)
-    total3, sent3 = send(msg3, part3, 8 * blocks, a3s, a3r)
-
-    c2 = coefficients(total2())
-    for z in range(HALO, HALO + cz):
-        v = [own2(k, z) for k in range(5)]
-        x = sol[z - HALO]
-        r = v[0]
-        for k in range(4):
-            x = x + c2[k] * v[k]
-            r = r - (7.0 * c2[k]) * (v[k + 1] + v[k])
-        sol[z - HALO] = x
-        res[z - HALO] = r
+            coeffs[repeat, k : k + 1, :] = c[k]
+        for z in range(HALO, HALO + cz):
+            v = [own(k, z) for k in range(5)]
+            x = sol[z - HALO]
+            r = v[0]
+            for k in range(4):
+                x = x + c[k] * v[k]
+                r = r - (7.0 * c[k]) * (v[k + 1] + v[k])
+            sol[z - HALO] = x
+            res[z - HALO] = r
+
+        @pl.when(repeat == 0)
+        def _():
+            ext[2, own_z, own_y, :] = res[...]
+            halo_start(ext, (2,), h2s, h2r)
+            halo_recv(ext, (2,), h2s, h2r)
+
+        return carry
+
+    lax.fori_loop(0, 2, one_block, 0)
 
     lane1 = lax.broadcasted_iota(jnp.int32, (1, nx), 1)
     scale = 1.0 / (float(count * inlets) ** 0.5)
-    sums = total3()
-    contrib = []
-    for at in range(blocks):
-        value = sums[at * 8 : at * 8 + 1, :]
+    contrib = [0.0] * blocks
+    for repeat in range(2):
+        sums = inlet(repeat)[1]()
         for k in range(4):
-            value = value + c2[k] * sums[at * 8 + 1 + k : at * 8 + 2 + k, :]
-        contrib.append(value)
+            for at in range(blocks):
+                row = k * blocks + at
+                contrib[at] = (
+                    contrib[at] + coeffs[repeat, k : k + 1, :] * sums[row : row + 1, :]
+                )
     for load in loads[3:]:
         load.wait()
     row = jnp.zeros((1, nx), jnp.float32)
@@ -360,9 +355,11 @@
         row = jnp.where(lane1 == j, conduct[j] * (header * scale - level[j]), row)
     flow[...] = row[:, :per]
 
-    sent2()
-    sent3()
-    halo_sent(ext2, (), h2s, h2r)
+    for repeat in range(2):
+        grams(repeat)[2]()
+        inlet(repeat)[2]()
+    halo_sent(ext, (pl.ds(0, 2),), h1s, h1r)
+    halo_sent(ext, (2,), h2s, h2r)
 
 
 def deliver(sol, res, flow, sol_out, res_out, flow_out, sems):
@@ -383,7 +380,7 @@
     per = conductance.shape[0]
     z_all, y_all = cz + 2 * HALO, cy + 2 * PAD
     count = n_slab * n_tile
-    rows3 = 8 * -(-plates // nx)
+    rows2 = 8 * -(-4 * -(-plates // nx) // 8)
     f32, i32 = jnp.float32, jnp.int32
     block = jax.ShapeDtypeStruct((cz, cy, nx), f32)
     shapes = (block, block, jax.ShapeDtypeStruct((1, per), f32))
@@ -394,26 +391,23 @@
         in_specs=[ANY] * 6,
         out_specs=(VMEM,) * 3,
         scratch_shapes=[
-            pltpu.VMEM((2, z_all, y_all, nx), f32),
-            pltpu.VMEM((4, z_all, y_all, nx), f32),
-            pltpu.VMEM((z_all, y_all, nx), f32),
+            pltpu.VMEM((3, z_all, y_all, nx), f32),
             pltpu.VMEM((4, z_all, y_all, nx), f32),
             pltpu.VMEM((z_all, y_all, nx), f32),
             pltpu.VMEM((z_all, y_all, nx), f32),
             pltpu.VMEM((inlets, plates), i32),
             pltpu.VMEM((inlets, plates, 2 * nx), jnp.bfloat16),
             pltpu.VMEM((inlets, plates, nx), f32),
+            pltpu.VMEM((2, 8, nx), f32),
             pltpu.SMEM(plate_order.shape, i32),
             pltpu.SMEM((per,), f32),
             pltpu.SMEM((per,), f32),
-            pltpu.VMEM((8, nx), f32),
-            pltpu.VMEM((count, 8, nx), f32),
-            pltpu.VMEM((8, nx), f32),
-            pltpu.VMEM((count, 8, nx), f32),
-            pltpu.VMEM((rows3, nx), f32),
-            pltpu.VMEM((count, rows3, nx), f32),
+            pltpu.VMEM((2, 8, nx), f32),
+            pltpu.VMEM((2, count, 8, nx), f32),
+            pltpu.VMEM((2, rows2, nx), f32),
+            pltpu.VMEM((2, count, rows2, nx), f32),
             dma((8,)), dma((8,)), dma((8,)), dma((8,)),
-            dma, dma, dma, dma, dma, dma, dma((6,)),
+            dma((2,)), dma((2,)), dma((2,)), dma((2,)), dma((6,)),
         ],
         compiler_params=pltpu.CompilerParams(
             collective_id=0, has_side_effects=True, vmem_limit_bytes=60 * 1024 * 1024

time: 27.6 us -> 26.9 us (0.975)
  Pallas kernels: 26.8 us -> 26.1 us
    pallas_call x1, Pallas kernels: 26.1 us -> 25.4 us  [on_device(): pl.pallas_call(functools.partial(kernel, n_slab, n_tile), out_shape=tuple...]
where the time goes in v4:
time: 26.9 us; the launch traced here: 26.7 us
  Pallas kernels  26.1 us (97%)
  between operations  0.64 us (2%)
    pallas_call x1, Pallas kernels, on_device(): pl.pallas_call(functools.partial(kernel, n_slab, n_tile), out_shape=tuple...  25.4 us
    pallas_call x1, Pallas kernels, on_device(): pl.pallas_call(deliver, out_shape=shapes, in_specs=[VMEM] * 3, out_specs=...  0.68 us

profile of v4, /device:TPU:0, one launch (start us, length us, event | category | flops | bytes accessed | tf_op | source)
XLA Modules:
  0.0 26.7 jit_solution(5051611705728663200)
XLA Ops:
  0.6 25.4 %shard_map.85 = (f32[8,16,128]{2,1,0:T(8,128)S(1)}, f32[8,16,128]{2,1,0:T(8,128)S(1)}, f32[1,4]{1,0:T(1,128)S(1)}) custom-call(f32[8,16,128]{2,1,0:T(8,128)} %rs.1, f32[8,16,128]{2,1,0:T(8,128)} %diag.1, s32[1,1,16,32]{3,2,1,0:T(8,128)} %bitcast.2, s32[32]{0:T(128)} %order_in.1, f32[4]{0:T(128)} %conduct_in.1, f32[4]{0:T(128)} %level_in.1), custom_call_target="tpu_custom_call" | custom-call | tf_op jit(solution)/shard_map/pallas_call | solution.py:388
  26.0 0.7 %shard_map.86 = (f32[8,16,128]{2,1,0:T(8,128)}, f32[8,16,128]{2,1,0:T(8,128)}, f32[1,4]{1,0:T(1,128)}) custom-call(f32[8,16,128]{2,1,0:T(8,128)S(1)} %get-tuple-element.9.sol, f32[8,16,128]{2,1,0:T(8,128)S(1)} %get-tuple-element.10.res, f32[1,4]{1,0:T(1,128)S(1)} %get-tuple-element.11.flow), custom_call_target="tpu_custom_call" | custom-call | tf_op jit(solution)/shard_map/pallas_call | solution.py:416

commit v5 on v4

--- a/solution.py
+++ b/solution.py
@@ -180,11 +180,14 @@
     spots = jnp.concatenate(
         [padded[:, at : at + nx].T for at in range(0, padded.shape[1], nx)], axis=0
     )[:plates]
+    spot_line = lax.div(spots, jnp.full_like(spots, nx))
+    spot_lane = spots - spot_line * nx
     for slot in range(inlets):
-        where = jnp.broadcast_to(spots[:, slot : slot + 1], (plates, nx))
-        line = jnp.where(where // nx == lanes, 1.0, 0.0).astype(jnp.bfloat16)
+        line = jnp.broadcast_to(spot_line[:, slot : slot + 1], (plates, nx)) == lanes
+        line = jnp.where(line, 1.0, 0.0).astype(jnp.bfloat16)
         first[slot] = jnp.concatenate([line, line], axis=1)
-        here[slot] = jnp.where(where % nx == lanes, 1.0, 0.0)
+        lane = jnp.broadcast_to(spot_lane[:, slot : slot + 1], (plates, nx)) == lanes
+        here[slot] = jnp.where(lane, 1.0, 0.0)
 
     for z in range(z_all):
         gz = me_s * cz + (z - HALO)
@@ -208,7 +211,11 @@
                     jnp.where(lane_at == 0, 0.0, pltpu.roll(c, 1, 1))
                     + jnp.where(lane_at == nx - 1, 0.0, pltpu.roll(c, nx - 1, 1))
                 )
-                store[k, z] = dm[z] * c - wt[z] * beside
+                made = dm[z] * c - wt[z] * beside
+                if k == STEPS - 1:
+                    store[k, z, own_y, :] = made[own_y]
+                else:
+                    store[k, z] = made
 
     def products(own):
         acc = [None] * len(PAIRS)
@@ -246,28 +253,28 @@
         return sums
 
     def send(msg, slots, at, rows, send_sem, recv_sem):
-        send_sem, recv_sem = send_sem.at[at], recv_sem.at[at]
+        send_sem, recv_sem = send_sem.at[at.start], recv_sem.at[at.start]
 
         def copy(device):
             return pltpu.make_async_remote_copy(
-                src_ref=msg.at[at, pl.ds(0, rows)], dst_ref=slots.at[at, me, pl.ds(0, rows)],
+                src_ref=msg.at[at, pl.ds(0, rows)], dst_ref=slots.at[me, at, pl.ds(0, rows)],
                 send_sem=send_sem, recv_sem=recv_sem,
                 device_id=device, device_id_type=MESH,
             )
 
-        others = slots.at[at, pl.ds(0, count - 1), pl.ds(0, rows)]
+        others = slots.at[pl.ds(0, count - 1), at, pl.ds(0, rows)]
         every = pltpu.make_async_remote_copy(
             src_ref=others, dst_ref=others, send_sem=send_sem, recv_sem=recv_sem,
             device_id=place(1), device_id_type=MESH,
         )
         def start():
             every_other(lambda device: copy(device).start())
-            slots[at, me, 0:rows, :] = msg[at, 0:rows, :]
+            slots[me, at, 0:rows, :] = msg[at, 0:rows, :]
 
         def total():
             every.wait_recv()
             if count <= 32:
-                parts = [slots[at, i, 0:rows, :] for i in range(count)]
+                parts = [slots[i, at, 0:rows, :] for i in range(count)]
                 while len(parts) > 1:
                     parts = [
                         parts[i] + parts[i + 1] if i + 1 < len(parts) else parts[i]
@@ -275,14 +282,14 @@
                     ]
                 return parts[0]
             return lax.fori_loop(
-                1, count, lambda i, t: t + slots[at, i, 0:rows, :], slots[at, 0, 0:rows, :]
+                1, count, lambda i, t: t + slots[i, at, 0:rows, :], slots[0, at, 0:rows, :]
             )
 
         return start, total, every.wait_send
 
     blocks = -(-plates // nx)
-    grams = lambda at: send(msg1, part1, at, 1, a1s, a1r)
-    inlet = lambda at: send(msg2, part2, at, 4 * blocks, a2s, a2r)
+    grams = lambda at: send(msg1, part1, pl.ds(at, 1), 1, a1s, a1r)
+    start2, total2, sent2 = send(msg2, part2, pl.ds(0, 2), 4 * blocks, a2s, a2r)
     sol[...] = jnp.zeros_like(sol)
 
     def one_block(repeat, carry):
@@ -307,9 +314,12 @@
             for at in range(blocks):
                 row = k * blocks + at
                 msg2[repeat, row : row + 1, :] = to_lanes(column, at * nx)
-        inlet(repeat)[0]()
-
-        c = coefficients(total())
+
+        @pl.when(repeat == 1)
+        def _():
+            start2()
+
+        c = coefficients(total()[0])
         for k in range(4):
             coeffs[repeat, k : k + 1, :] = c[k]
         for z in range(HALO, HALO + cz):
@@ -335,8 +345,9 @@
     lane1 = lax.broadcasted_iota(jnp.int32, (1, nx), 1)
     scale = 1.0 / (float(count * inlets) ** 0.5)
     contrib = [0.0] * blocks
+    inlet_total = total2()
     for repeat in range(2):
-        sums = inlet(repeat)[1]()
+        sums = inlet_total[repeat]
         for k in range(4):
             for at in range(blocks):
                 row = k * blocks + at
@@ -357,7 +368,7 @@
 
     for repeat in range(2):
         grams(repeat)[2]()
-        inlet(repeat)[2]()
+    sent2()
     halo_sent(ext, (pl.ds(0, 2),), h1s, h1r)
     halo_sent(ext, (2,), h2s, h2r)
 
@@ -403,9 +414,9 @@
             pltpu.SMEM((per,), f32),
             pltpu.SMEM((per,), f32),
             pltpu.VMEM((2, 8, nx), f32),
-            pltpu.VMEM((2, count, 8, nx), f32),
+            pltpu.VMEM((count, 2, 8, nx), f32),
             pltpu.VMEM((2, rows2, nx), f32),
-            pltpu.VMEM((2, count, rows2, nx), f32),
+            pltpu.VMEM((count, 2, rows2, nx), f32),
             dma((8,)), dma((8,)), dma((8,)), dma((8,)),
             dma((2,)), dma((2,)), dma((2,)), dma((2,)), dma((6,)),
         ],

time: 26.9 us -> 27.8 us (1.033)
  Pallas kernels: 26.1 us -> 27 us
    pallas_call x1, Pallas kernels: 25.4 us -> 26.3 us  [on_device(): pl.pallas_call(functools.partial(kernel, n_slab, n_tile), out_shape=tuple...]
where the time goes in v5:
time: 27.8 us; the launch traced here: 27.6 us
  Pallas kernels  27 us (97%)
  between operations  0.64 us (2%)
    pallas_call x1, Pallas kernels, on_device(): pl.pallas_call(functools.partial(kernel, n_slab, n_tile), out_shape=tuple...  26.3 us
    pallas_call x1, Pallas kernels, on_device(): pl.pallas_call(deliver, out_shape=shapes, in_specs=[VMEM] * 3, out_specs=...  0.68 us

profile of v5, /device:TPU:0, one launch (start us, length us, event | category | flops | bytes accessed | tf_op | source)
XLA Modules:
  0.0 27.6 jit_solution(17788219391502958362)
XLA Ops:
  0.6 26.3 %shard_map.85 = (f32[8,16,128]{2,1,0:T(8,128)S(1)}, f32[8,16,128]{2,1,0:T(8,128)S(1)}, f32[1,4]{1,0:T(1,128)S(1)}) custom-call(f32[8,16,128]{2,1,0:T(8,128)} %rs.1, f32[8,16,128]{2,1,0:T(8,128)} %diag.1, s32[1,1,16,32]{3,2,1,0:T(8,128)} %bitcast.2, s32[32]{0:T(128)} %order_in.1, f32[4]{0:T(128)} %conduct_in.1, f32[4]{0:T(128)} %level_in.1), custom_call_target="tpu_custom_call" | custom-call | tf_op jit(solution)/shard_map/pallas_call | solution.py:399
  26.9 0.7 %shard_map.86 = (f32[8,16,128]{2,1,0:T(8,128)}, f32[8,16,128]{2,1,0:T(8,128)}, f32[1,4]{1,0:T(1,128)}) custom-call(f32[8,16,128]{2,1,0:T(8,128)S(1)} %get-tuple-element.9.sol, f32[8,16,128]{2,1,0:T(8,128)S(1)} %get-tuple-element.10.res, f32[1,4]{1,0:T(1,128)S(1)} %get-tuple-element.11.flow), custom_call_target="tpu_custom_call" | custom-call | tf_op jit(solution)/shard_map/pallas_call | solution.py:427

commit v6 on v4

--- a/solution.py
+++ b/solution.py
@@ -37,10 +37,15 @@
     return c
 
 
-def to_lanes(column, at):
-    sub = lax.broadcasted_iota(jnp.int32, column.shape, 0)
-    lane = lax.broadcasted_iota(jnp.int32, column.shape, 1)
-    return jnp.sum(jnp.where(lane + at == sub, column, 0.0), axis=0, keepdims=True)
+def to_lanes(columns, at):
+    rows = columns[0].shape[0]
+    sub = lax.broadcasted_iota(jnp.int32, columns[0].shape, 0)
+    lane = lax.broadcasted_iota(jnp.int32, columns[0].shape, 1)
+    total = None
+    for k, column in enumerate(columns):
+        term = jnp.where(lane + (at - k * rows) == sub, column, 0.0)
+        total = term if total is None else total + term
+    return jnp.sum(total, axis=0, keepdims=True)
 
 
 def coefficients(row):
@@ -180,11 +185,14 @@
     spots = jnp.concatenate(
         [padded[:, at : at + nx].T for at in range(0, padded.shape[1], nx)], axis=0
     )[:plates]
+    spot_line = lax.div(spots, jnp.full_like(spots, nx))
+    spot_lane = spots - spot_line * nx
     for slot in range(inlets):
-        where = jnp.broadcast_to(spots[:, slot : slot + 1], (plates, nx))
-        line = jnp.where(where // nx == lanes, 1.0, 0.0).astype(jnp.bfloat16)
+        line = jnp.broadcast_to(spot_line[:, slot : slot + 1], (plates, nx)) == lanes
+        line = jnp.where(line, 1.0, 0.0).astype(jnp.bfloat16)
         first[slot] = jnp.concatenate([line, line], axis=1)
-        here[slot] = jnp.where(where % nx == lanes, 1.0, 0.0)
+        lane = jnp.broadcast_to(spot_lane[:, slot : slot + 1], (plates, nx)) == lanes
+        here[slot] = jnp.where(lane, 1.0, 0.0)
 
     for z in range(z_all):
         gz = me_s * cz + (z - HALO)
@@ -208,7 +216,11 @@
                     jnp.where(lane_at == 0, 0.0, pltpu.roll(c, 1, 1))
                     + jnp.where(lane_at == nx - 1, 0.0, pltpu.roll(c, nx - 1, 1))
                 )
-                store[k, z] = dm[z] * c - wt[z] * beside
+                made = dm[z] * c - wt[z] * beside
+                if k == STEPS - 1:
+                    store[k, z, own_y, :] = made[own_y]
+                else:
+                    store[k, z] = made
 
     def products(own):
         acc = [None] * len(PAIRS)
@@ -220,7 +232,7 @@
         rows = [jnp.sum(term, axis=0, keepdims=True) for term in acc]
         rows = jnp.concatenate(rows + [jnp.zeros((1, nx), jnp.float32)], axis=0)
         column = jnp.broadcast_to(jnp.sum(rows, axis=1, keepdims=True), rows.shape)
-        return to_lanes(column, 0)
+        return to_lanes([column], 0)
 
     def inlet_sums(fields):
         halves = []
@@ -280,9 +292,9 @@
 
         return start, total, every.wait_send
 
-    blocks = -(-plates // nx)
+    blocks = -(-4 * plates // nx)
     grams = lambda at: send(msg1, part1, at, 1, a1s, a1r)
-    inlet = lambda at: send(msg2, part2, at, 4 * blocks, a2s, a2r)
+    inlet = lambda at: send(msg2, part2, at, blocks, a2s, a2r)
     sol[...] = jnp.zeros_like(sol)
 
     def one_block(repeat, carry):
@@ -303,10 +315,8 @@
             jnp.concatenate([own(k, z) for z in range(HALO, HALO + cz)], axis=0)
             for k in range(4)
         ])
-        for k, column in enumerate(picked):
-            for at in range(blocks):
-                row = k * blocks + at
-                msg2[repeat, row : row + 1, :] = to_lanes(column, at * nx)
+        for at in range(blocks):
+            msg2[repeat, at : at + 1, :] = to_lanes(picked, at * nx)
         inlet(repeat)[0]()
 
         c = coefficients(total())
@@ -337,12 +347,13 @@
     contrib = [0.0] * blocks
     for repeat in range(2):
         sums = inlet(repeat)[1]()
-        for k in range(4):
-            for at in range(blocks):
-                row = k * blocks + at
-                contrib[at] = (
-                    contrib[at] + coeffs[repeat, k : k + 1, :] * sums[row : row + 1, :]
-                )
+        for at in range(blocks):
+            spot = lane1 + at * nx
+            weight = coeffs[repeat, 3:4, :]
+            for k in (2, 1, 0):
+                weight = jnp.where(spot < (k + 1) * plates, coeffs[repeat, k : k + 1, :], weight)
+            weight = jnp.where(spot < 4 * plates, weight, 0.0)
+            contrib[at] = contrib[at] + weight * sums[at : at + 1, :]
     for load in loads[3:]:
         load.wait()
     row = jnp.zeros((1, nx), jnp.float32)
@@ -350,7 +361,9 @@
         plate = order[me_t * per + j]
         header = jnp.zeros((1, nx), jnp.float32)
         for at in range(blocks):
-            header = header + jnp.where(lane1 + at * nx == plate, contrib[at], 0.0)
+            for k in range(4):
+                mine = lane1 + at * nx == plate + k * plates
+                header = header + jnp.where(mine, contrib[at], 0.0)
         header = jnp.sum(header, axis=1, keepdims=True)
         row = jnp.where(lane1 == j, conduct[j] * (header * scale - level[j]), row)
     flow[...] = row[:, :per]
@@ -380,7 +393,7 @@
     per = conductance.shape[0]
     z_all, y_all = cz + 2 * HALO, cy + 2 * PAD
     count = n_slab * n_tile
-    rows2 = 8 * -(-4 * -(-plates // nx) // 8)
+    rows2 = 8 * -(-4 * plates // (8 * nx))
     f32, i32 = jnp.float32, jnp.int32
     block = jax.ShapeDtypeStruct((cz, cy, nx), f32)
     shapes = (block, block, jax.ShapeDtypeStruct((1, per), f32))

time: 26.9 us -> 26.5 us (0.985)
  Pallas kernels: 26.1 us -> 25.7 us
    pallas_call x1, Pallas kernels: 25.4 us -> 25 us  [on_device(): pl.pallas_call(functools.partial(kernel, n_slab, n_tile), out_shape=tuple...]
where the time goes in v6:
time: 26.5 us; the launch traced here: 26.3 us
  Pallas kernels  25.7 us (97%)
  between operations  0.64 us (2%)
    pallas_call x1, Pallas kernels, on_device(): pl.pallas_call(functools.partial(kernel, n_slab, n_tile), out_shape=tuple...  25 us
    pallas_call x1, Pallas kernels, on_device(): pl.pallas_call(deliver, out_shape=shapes, in_specs=[VMEM] * 3, out_specs=...  0.68 us

profile of v6, /device:TPU:0, one launch (start us, length us, event | category | flops | bytes accessed | tf_op | source)
XLA Modules:
  0.0 26.3 jit_solution(15703023652986109549)
XLA Ops:
  0.6 25.0 %shard_map.85 = (f32[8,16,128]{2,1,0:T(8,128)S(1)}, f32[8,16,128]{2,1,0:T(8,128)S(1)}, f32[1,4]{1,0:T(1,128)S(1)}) custom-call(f32[8,16,128]{2,1,0:T(8,128)} %rs.1, f32[8,16,128]{2,1,0:T(8,128)} %diag.1, s32[1,1,16,32]{3,2,1,0:T(8,128)} %bitcast.2, s32[32]{0:T(128)} %order_in.1, f32[4]{0:T(128)} %conduct_in.1, f32[4]{0:T(128)} %level_in.1), custom_call_target="tpu_custom_call" | custom-call | tf_op jit(solution)/shard_map/pallas_call | solution.py:401
  25.6 0.7 %shard_map.86 = (f32[8,16,128]{2,1,0:T(8,128)}, f32[8,16,128]{2,1,0:T(8,128)}, f32[1,4]{1,0:T(1,128)}) custom-call(f32[8,16,128]{2,1,0:T(8,128)S(1)} %get-tuple-element.9.sol, f32[8,16,128]{2,1,0:T(8,128)S(1)} %get-tuple-element.10.res, f32[1,4]{1,0:T(1,128)S(1)} %get-tuple-element.11.flow), custom_call_target="tpu_custom_call" | custom-call | tf_op jit(solution)/shard_map/pallas_call | solution.py:429

commit v7 on v6

--- a/solution.py
+++ b/solution.py
@@ -71,9 +71,9 @@
 def kernel(
     n_slab, n_tile, rs, diag, index, order_in, conduct_in, level_in,
     sol, res, flow,
-    ext, basis, dm, wt, cells, first, here, coeffs,
-    order, conduct, level, msg1, part1, msg2, part2,
-    h1s, h1r, h2s, h2r, a1s, a1r, a2s, a2r, local,
+    ext, basis, dm, wt, cells, first, here, coeffs, everything,
+    order, conduct, level, msg, part,
+    h1s, h1r, h2s, h2r, a1s, a1r, local,
 ):
     cz, cy, nx = rs.shape
     inlets, plates = index.shape[2], index.shape[3]
@@ -293,8 +293,9 @@
         return start, total, every.wait_send
 
     blocks = -(-4 * plates // nx)
-    grams = lambda at: send(msg1, part1, at, 1, a1s, a1r)
-    inlet = lambda at: send(msg2, part2, at, blocks, a2s, a2r)
+    rows = 1 + 2 * blocks
+    sums = lambda at: send(msg, part, at, rows, a1s, a1r)
+    msg[...] = jnp.zeros_like(msg)
     sol[...] = jnp.zeros_like(sol)
 
     def one_block(repeat, carry):
@@ -307,19 +308,30 @@
             return ext[v0, z, own_y, :] if k == 0 else basis[k - 1, z, own_y, :]
 
         powers(read, basis)
-        msg1[repeat, 0:1, :] = products(own)
-        start, total, _ = grams(repeat)
+        msg[repeat, 0:1, :] = products(own)
+
+        def pick(first_row):
+            picked = inlet_sums([
+                jnp.concatenate([own(k, z) for z in range(HALO, HALO + cz)], axis=0)
+                for k in range(4)
+            ])
+            for at in range(blocks):
+                row = first_row + at
+                msg[1, row : row + 1, :] = to_lanes(picked, at * nx)
+
+        @pl.when(repeat == 1)
+        def _():
+            pick(1 + blocks)
+
+        start, total, _ = sums(repeat)
         start()
 
-        picked = inlet_sums([
-            jnp.concatenate([own(k, z) for z in range(HALO, HALO + cz)], axis=0)
-            for k in range(4)
-        ])
-        for at in range(blocks):
-            msg2[repeat, at : at + 1, :] = to_lanes(picked, at * nx)
-        inlet(repeat)[0]()
-
-        c = coefficients(total())
+        @pl.when(repeat == 0)
+        def _():
+            pick(1)
+
+        everything[...] = total()
+        c = coefficients(everything[0:1, :])
         for k in range(4):
             coeffs[repeat, k : k + 1, :] = c[k]
         for z in range(HALO, HALO + cz):
@@ -346,14 +358,14 @@
     scale = 1.0 / (float(count * inlets) ** 0.5)
     contrib = [0.0] * blocks
     for repeat in range(2):
-        sums = inlet(repeat)[1]()
         for at in range(blocks):
             spot = lane1 + at * nx
             weight = coeffs[repeat, 3:4, :]
             for k in (2, 1, 0):
                 weight = jnp.where(spot < (k + 1) * plates, coeffs[repeat, k : k + 1, :], weight)
             weight = jnp.where(spot < 4 * plates, weight, 0.0)
-            contrib[at] = contrib[at] + weight * sums[at : at + 1, :]
+            row = 1 + repeat * blocks + at
+            contrib[at] = contrib[at] + weight * everything[row : row + 1, :]
     for load in loads[3:]:
         load.wait()
     row = jnp.zeros((1, nx), jnp.float32)
@@ -369,8 +381,7 @@
     flow[...] = row[:, :per]
 
     for repeat in range(2):
-        grams(repeat)[2]()
-        inlet(repeat)[2]()
+        sums(repeat)[2]()
     halo_sent(ext, (pl.ds(0, 2),), h1s, h1r)
     halo_sent(ext, (2,), h2s, h2r)
 
@@ -393,7 +404,8 @@
     per = conductance.shape[0]
     z_all, y_all = cz + 2 * HALO, cy + 2 * PAD
     count = n_slab * n_tile
-    rows2 = 8 * -(-4 * plates // (8 * nx))
+    rows = 1 + 2 * -(-4 * plates // nx)
+    rows2 = 8 * -(-rows // 8)
     f32, i32 = jnp.float32, jnp.int32
     block = jax.ShapeDtypeStruct((cz, cy, nx), f32)
     shapes = (block, block, jax.ShapeDtypeStruct((1, per), f32))
@@ -412,15 +424,14 @@
             pltpu.VMEM((inlets, plates, 2 * nx), jnp.bfloat16),
             pltpu.VMEM((inlets, plates, nx), f32),
             pltpu.VMEM((2, 8, nx), f32),
+            pltpu.VMEM((rows, nx), f32),
             pltpu.SMEM(plate_order.shape, i32),
             pltpu.SMEM((per,), f32),
             pltpu.SMEM((per,), f32),
-            pltpu.VMEM((2, 8, nx), f32),
-            pltpu.VMEM((2, count, 8, nx), f32),
             pltpu.VMEM((2, rows2, nx), f32),
             pltpu.VMEM((2, count, rows2, nx), f32),
             dma((8,)), dma((8,)), dma((8,)), dma((8,)),
-            dma((2,)), dma((2,)), dma((2,)), dma((2,)), dma((6,)),
+            dma((2,)), dma((2,)), dma((6,)),
         ],
         compiler_params=pltpu.CompilerParams(
             collective_id=0, has_side_effects=True, vmem_limit_bytes=60 * 1024 * 1024

time: 26.5 us -> 27 us (1.019)
  Pallas kernels: 25.7 us -> 26.2 us
    pallas_call x1, Pallas kernels: 25 us -> 25.5 us  [on_device(): pl.pallas_call(functools.partial(kernel, n_slab, n_tile), out_shape=tuple...]
where the time goes in v7:
time: 27 us; the launch traced here: 26.8 us
  Pallas kernels  26.2 us (97%)
  between operations  0.64 us (2%)
    pallas_call x1, Pallas kernels, on_device(): pl.pallas_call(functools.partial(kernel, n_slab, n_tile), out_shape=tuple...  25.5 us
    pallas_call x1, Pallas kernels, on_device(): pl.pallas_call(deliver, out_shape=shapes, in_specs=[VMEM] * 3, out_specs=...  0.68 us

profile of v7, /device:TPU:0, one launch (start us, length us, event | category | flops | bytes accessed | tf_op | source)
XLA Modules:
  0.0 26.8 jit_solution(16619724460276446491)
XLA Ops:
  0.6 25.5 %shard_map.85 = (f32[8,16,128]{2,1,0:T(8,128)S(1)}, f32[8,16,128]{2,1,0:T(8,128)S(1)}, f32[1,4]{1,0:T(1,128)S(1)}) custom-call(f32[8,16,128]{2,1,0:T(8,128)} %rs.1, f32[8,16,128]{2,1,0:T(8,128)} %diag.1, s32[1,1,16,32]{3,2,1,0:T(8,128)} %bitcast.2, s32[32]{0:T(128)} %order_in.1, f32[4]{0:T(128)} %conduct_in.1, f32[4]{0:T(128)} %level_in.1), custom_call_target="tpu_custom_call" | custom-call | tf_op jit(solution)/shard_map/pallas_call | solution.py:413
  26.1 0.7 %shard_map.86 = (f32[8,16,128]{2,1,0:T(8,128)}, f32[8,16,128]{2,1,0:T(8,128)}, f32[1,4]{1,0:T(1,128)}) custom-call(f32[8,16,128]{2,1,0:T(8,128)S(1)} %get-tuple-element.9.sol, f32[8,16,128]{2,1,0:T(8,128)S(1)} %get-tuple-element.10.res, f32[1,4]{1,0:T(1,128)S(1)} %get-tuple-element.11.flow), custom_call_target="tpu_custom_call" | custom-call | tf_op jit(solution)/shard_map/pallas_call | solution.py:440
